TPU v7x, 32 devices: a whole 2x2x4 slice. The times are simulated.
32 devices in a mesh: grp: 2 (over y), tp: 4 (over z), pd: 4 (over x, core).
Axes of the slice: x: 2, y: 2, z: 4, core: 2. Of those that a mesh axis runs over, the one named last changes fastest.
Arguments:
- x_attn: bfloat16 [2048, 8192], P(('grp', 'pd'), 'tp'), parts along dimension 0, may hold values from -16 to 16
- w_query: bfloat16 [8192, 8192], P(None, 'tp'), may hold values from -0.0625 to 0.0625
- w_keyval: bfloat16 [8192, 2048], replicated, may hold values from -0.0625 to 0.0625
- cache_pool: bfloat16 [8, 64, 16, 2048], P(('grp', 'pd'), 'tp'), parts along dimension 0, may hold values from -8 to 8
- page_table: int32 [8, 64], P(('grp', 'pd')), parts along dimension 0, may hold values from 0 to 63, each once within a row
- cached_len: int32 [8], P(('grp', 'pd')), parts along dimension 0, may hold values from 256 to 1024, as said below
- page_dest: int32 [8, 16, 1], P(('grp', 'pd')), parts along dimension 0, may hold values from 0 to 3; in each aligned block of 16 rows (0 to 15, 16 to 31, ..., all dimensions but the last counted through in order) at most 8 rows name the same one
- mamba_in: bfloat16 [2048, 16384], P(('grp', 'pd'), 'tp'), parts along dimension 0, may hold values from -6 to 6
- gate_in: bfloat16 [2048, 16384], P(('grp', 'pd'), 'tp'), parts along dimension 0, may hold values from -6 to 6
- conv_prev: bfloat16 [8, 3, 16384], P(('grp', 'pd'), None, 'tp'), parts along dimension 0, may hold values from -6 to 6
- state_prev: float32 [8, 16, 16384], P(('grp', 'pd'), None, 'tp'), parts along dimension 0, may hold values from -6 to 6
- conv_weight: float32 [4, 16384], P(None, 'tp'), may hold values from -0.8 to 0.8
- conv_bias: float32 [16384], P('tp'), may hold values from -0.5 to 0.5
- w_xdt: bfloat16 [16384, 512], P('tp'), may hold values from -0.046875 to 0.046875
- w_bc: bfloat16 [16384, 32], P('tp'), may hold values from -0.09375 to 0.09375
- w_dt: bfloat16 [512, 16384], P(None, 'tp'), may hold values from -0.25 to 0.25
- dt_bias: float32 [16384], P('tp'), may hold values from -6 to -1
- a_log: float32 [16, 16384], P(None, 'tp'), may hold values from -3 to 2.8
- d_skip: float32 [16384], P('tp'), may hold values from 0.5 to 1.5
Outputs:
- attn_out: bfloat16 [2048, 8192], P(('grp', 'pd'), 'tp'), parts along dimension 0
- decode_pages: bfloat16 [8, 32, 16, 2048], P(('grp', 'pd'), 'tp'), parts along dimension 0
- mamba_out: bfloat16 [2048, 16384], P(('grp', 'pd'), 'tp'), parts along dimension 0
- final_state: float32 [8, 16, 16384], P(('grp', 'pd'), None, 'tp'), parts along dimension 0
There are 2 independent parts, one for each index of `grp`. A program takes and returns all parts, laid end to end along the dimension named above; an argument that names none is the same for every part. Nothing has to cross between parts.
Inputs may be any that keep to these rules, and one draw needn't show every extreme that they name: `page_table`: row p is a permutation: entry j names the pool slot that holds logical cached page j of prompt p. `cached_len`: some prompt has exactly 1024 cached tokens. `page_dest`: within one prompt no device receives more than 8 new pages, and some device receives exactly 8.
All inputs are finite; a program needn't handle non-finite values.
Results may differ from a plain program's by a relative error of at most 0.017.
Values may be sent and summed in bfloat16 or wider, within the bound.
A program may use at most 512 MiB of HBM per device.

v0:
```python
import math

import jax
import jax.numpy as jnp
from jax import lax
from jax.sharding import PartitionSpec as P

HEADS = 64
KV_HEADS = 8
HEAD_DIM = 128
PAGE = 16


def block_part(query, key_rows, value_rows, usable):
    scores = jnp.einsum(
        "ckgd,lkd->ckgl", query, key_rows, preferred_element_type=jnp.float32
    ) / math.sqrt(HEAD_DIM)
    scores = jnp.where(usable[:, None, None, :], scores, -1e30)
    highest = jnp.max(scores, axis=-1)
    weights = jnp.where(usable[:, None, None, :], jnp.exp(scores - highest[..., None]), 0.0)
    totals = jnp.sum(weights, axis=-1)
    mixture = jnp.einsum(
        "ckgl,lkd->ckgd",
        weights.astype(jnp.bfloat16),
        value_rows,
        preferred_element_type=jnp.float32,
    )
    return (mixture, highest, totals)


def token_usable(page_map, slot_ids, length):
    logical = jnp.sum(
        jnp.where(
            page_map[None, :] == slot_ids[:, None], jnp.arange(page_map.shape[0])[None, :], 0
        ),
        axis=1,
    )
    positions = logical[:, None] * PAGE + jnp.arange(PAGE)[None, :]
    return (positions < length).reshape(-1)


def body(
    x_attn,
    w_query,
    w_keyval,
    cache_pool,
    page_table,
    cached_len,
    page_dest,
    mamba_in,
    gate_in,
    conv_prev,
    state_prev,
    conv_weight,
    conv_bias,
    w_xdt,
    w_bc,
    w_dt,
    dt_bias,
    a_log,
    d_skip,
):
    tp_size = lax.axis_size("tp")
    tp_index = lax.axis_index("tp")
    token_count = x_attn.shape[0]
    own_heads = w_query.shape[1] // HEAD_DIM
    group_size = HEADS // KV_HEADS
    own_groups = max(1, own_heads // group_size)
    per_group = own_heads // own_groups
    head_cols = 2 * HEAD_DIM
    kv_cols = w_keyval.shape[1]
    slice_cols = kv_cols // tp_size
    first_group = tp_index * own_heads // group_size
    w_own = lax.dynamic_slice_in_dim(w_keyval, first_group * head_cols, own_groups * head_cols, 1)
    piece = lax.all_gather(x_attn, "tp", axis=1, tiled=True)
    query_sum = jnp.dot(piece, w_query, preferred_element_type=jnp.float32)
    keyval_sum = jnp.dot(piece, w_own, preferred_element_type=jnp.float32)
    queries = query_sum.astype(jnp.bfloat16)
    fresh = keyval_sum.astype(jnp.bfloat16)
    page_count = token_count // PAGE
    capacity = max(2, 2 * page_count // tp_size)
    target = page_dest[0, :, 0]
    page_ids = jnp.arange(page_count)
    earlier = (target[None, :] == target[:, None]) & (page_ids[None, :] < page_ids[:, None])
    ranking = jnp.sum(earlier.astype(jnp.int32), axis=1)
    slot_ids = jnp.arange(capacity)
    my_slice = lax.dynamic_slice_in_dim(
        fresh, tp_index * slice_cols - first_group * head_cols, slice_cols, 1
    )
    pieces_out = my_slice.reshape(page_count, PAGE * slice_cols)
    onehot = (
        (target[None, None, :] == jnp.arange(tp_size)[:, None, None])
        & (ranking[None, None, :] == slot_ids[None, :, None])
    ).astype(jnp.bfloat16)
    outgoing = jnp.einsum(
        "drj,jx->drx", onehot, pieces_out, preferred_element_type=jnp.float32
    ).astype(jnp.bfloat16)
    arrived = lax.all_to_all(outgoing, "tp", split_axis=0, concat_axis=2, tiled=True)
    decode = (
        arrived.reshape(capacity, tp_size, PAGE, slice_cols)
        .transpose(0, 2, 1, 3)
        .reshape(1, capacity, PAGE, kv_cols)
    )
    query_own = queries.reshape(token_count, own_groups, per_group, HEAD_DIM)
    new_kv = fresh.reshape(token_count, own_groups, 2, HEAD_DIM)
    token_ids = jnp.arange(token_count)
    causal = token_ids[:, None] >= token_ids[None, :]
    running = block_part(query_own, new_kv[:, :, 0], new_kv[:, :, 1], causal)
    length = cached_len[0]
    page_map = page_table[0]
    local_slots = cache_pool.shape[1]
    page_pool = cache_pool[0]
    everyone = lax.all_gather(queries, "tp", axis=1, tiled=True)
    local_ids = tp_index * local_slots + jnp.arange(local_slots)
    usable = token_usable(page_map, local_ids, length)
    masking = jnp.broadcast_to(usable[None, :], (token_count, usable.shape[0]))
    local_pool = page_pool.reshape(local_slots * PAGE, KV_HEADS, 2, HEAD_DIM)
    query_all = everyone.reshape(token_count, KV_HEADS, group_size, HEAD_DIM)

    def head_part(operands):
        query_head, key_head, value_head = operands
        return block_part(query_head[:, None], key_head[:, None], value_head[:, None], masking)

    partial_value = lax.map(
        head_part,
        (
            jnp.moveaxis(query_all, 1, 0),
            jnp.moveaxis(local_pool[:, :, 0], 1, 0),
            jnp.moveaxis(local_pool[:, :, 1], 1, 0),
        ),
    )
    far_mix = jnp.moveaxis(partial_value[0][:, :, 0], 0, 1).reshape(token_count, HEADS * HEAD_DIM)
    far_high = jnp.moveaxis(partial_value[1][:, :, 0], 0, 1).reshape(token_count, HEADS)
    far_total = jnp.moveaxis(partial_value[2][:, :, 0], 0, 1).reshape(token_count, HEADS)
    back_mix, back_high, back_total = (
        lax.all_to_all(
            far_mix.astype(jnp.bfloat16), "tp", split_axis=1, concat_axis=0, tiled=True
        ).astype(far_mix.dtype),
        lax.all_to_all(
            far_high.astype(jnp.bfloat16), "tp", split_axis=1, concat_axis=0, tiled=True
        ).astype(far_high.dtype),
        lax.all_to_all(
            far_total.astype(jnp.bfloat16), "tp", split_axis=1, concat_axis=0, tiled=True
        ).astype(far_total.dtype),
    )
    back_mix = back_mix.reshape(tp_size, token_count, own_groups, per_group, HEAD_DIM)
    back_high = back_high.reshape(tp_size, token_count, own_groups, per_group)
    back_total = back_total.reshape(tp_size, token_count, own_groups, per_group)
    mixture, highest, totals = running
    peak = jnp.maximum(highest, jnp.max(back_high, axis=0))
    nearby = jnp.exp(highest - peak)
    remote = jnp.exp(back_high - peak[None])
    mixture = mixture * nearby[..., None] + jnp.sum(back_mix * remote[..., None], axis=0)
    totals = totals * nearby + jnp.sum(back_total * remote, axis=0)
    attn_out = (
        (mixture / totals[..., None])
        .astype(jnp.bfloat16)
        .reshape(token_count, own_heads * HEAD_DIM)
    )
    extended = jnp.concatenate([conv_prev[0], mamba_in], axis=0).astype(jnp.float32)
    convolved = jnp.broadcast_to(conv_bias[None, :], mamba_in.shape)
    for offset in range(conv_weight.shape[0]):
        convolved = (
            convolved + conv_weight[offset][None, :] * extended[offset : offset + token_count]
        )
    xconv = jax.nn.silu(convolved).astype(jnp.bfloat16)
    proj_part = jnp.dot(xconv, w_xdt, preferred_element_type=jnp.float32)
    select_part = jnp.dot(xconv, w_bc, preferred_element_type=jnp.float32)
    projected, selection = (
        lax.psum(proj_part.astype(jnp.bfloat16), "tp").astype(jnp.float32),
        lax.psum(select_part.astype(jnp.bfloat16), "tp").astype(jnp.float32),
    )
    low_norm = (
        projected * lax.rsqrt(jnp.mean(projected * projected, axis=-1, keepdims=True) + 1e-06)
    ).astype(jnp.bfloat16)
    step_size = jax.nn.softplus(
        jnp.dot(low_norm, w_dt, preferred_element_type=jnp.float32) + dt_bias[None, :]
    )
    decay_rate = -jnp.exp(a_log)
    state_size = a_log.shape[0]
    channels = a_log.shape[1]
    xconv_f = xconv.astype(jnp.float32)
    decay = jnp.exp(step_size[:, None, :] * decay_rate[None])
    push = (step_size * xconv_f)[:, None, :] * selection[:, :state_size, None]
    block_len = min(16, token_count)
    block_count = token_count // block_len

    def scan_block(state, pieces):
        decay_block, push_block, read_block = pieces

        def combine(former, latter):
            return (former[0] * latter[0], latter[0] * former[1] + latter[1])

        cum_decay, cum_push = lax.associative_scan(combine, (decay_block, push_block), axis=0)
        states = cum_decay * state[None] + cum_push
        return (states[-1], jnp.sum(read_block[:, :, None] * states, axis=1))

    last_state, readout = lax.scan(
        scan_block,
        state_prev[0],
        (
            decay.reshape(block_count, block_len, state_size, channels),
            push.reshape(block_count, block_len, state_size, channels),
            selection[:, state_size:].reshape(block_count, block_len, state_size),
        ),
    )
    readout = readout.reshape(token_count, channels) + d_skip[None, :] * xconv_f
    mamba_out = (readout * jax.nn.silu(gate_in.astype(jnp.float32))).astype(jnp.bfloat16)
    return (attn_out, decode, mamba_out, last_state[None])


def solution(mesh):
    return jax.shard_map(
        body,
        mesh=mesh,
        in_specs=(
            P(("grp", "pd"), "tp"),
            P(None, "tp"),
            P(),
            P(("grp", "pd"), "tp", None, None),
            P(("grp", "pd"), None),
            P(("grp", "pd")),
            P(("grp", "pd"), None, None),
            P(("grp", "pd"), "tp"),
            P(("grp", "pd"), "tp"),
            P(("grp", "pd"), None, "tp"),
            P(("grp", "pd"), None, "tp"),
            P(None, "tp"),
            P("tp"),
            P("tp", None),
            P("tp", None),
            P(None, "tp"),
            P("tp"),
            P(None, "tp"),
            P("tp"),
        ),
        out_specs=(
            P(("grp", "pd"), "tp"),
            P(("grp", "pd"), "tp", None, None),
            P(("grp", "pd"), "tp"),
            P(("grp", "pd"), None, "tp"),
        ),
        check_vma=False,
    )
```

profile of v0, /device:TPU:0, one launch (start us, length us, event | category | flops | bytes accessed | tf_op | source)
XLA Modules:
  0.0 2051.0 jit_solution(12575444637702910636)
XLA Ops:
  17.1 76.0 %all-gather.3.cloned.1.call-done = bf16[256,8192]{1,0:T(8,128)(2,1)} async-done(((bf16[256,2048]{1,0:T(8,128)(2,1)}), bf16[256,8192]{1,0:T(8,128)(2,1)}) %all-gather.3.cloned.1.call-update) | async-done | bytes 4194320 | tf_op jit(solution)/shard_map/all_gather | solution.py:75
  93.1 17.1 convolution_convert_fusion.1
  121.3 16.2 psum.15
  141.1 9.1 convert_multiply_fusion.2
  161.6 61.0 %all-gather.5.cloned.1.call-done = bf16[256,8192]{1,0:T(8,128)(2,1)} async-done(((bf16[256,2048]{1,0:T(8,128)(2,1)}), bf16[256,8192]{1,0:T(8,128)(2,1)}) %all-gather.5.cloned.1.call-update) | async-done | bytes 4194320 | tf_op jit(solution)/shard_map/all_gather | solution.py:113
  230.7 45.0 %while.28 = (s32[]{:T(128)}, bf16[8,256,1,8,128]{1,4,3,2,0:T(8,128)(2,1)}, bf16[8,256,1,8]{1,3,2,0:T(8,128)(2,1)}, bf16[8,256,1,8]{1,3,2,0:T(8,128)(2,1)}, bf16[...) while((s32[]{:T(128)}, ...), condition=%wide.region_5.6_spmd.clone, body=%wide.region_2.5_spmd.clone.sunk | while | flops 275247104 | bytes 8051821 | solution.py:124
  279.0 22.8 %broadcast_multiply_fusion = f32[16,16,16,4096]{3,2,1,0:T(8,128)} fusion(f32[16,16,16]{2,1,0:T(8,128)S(1)} %bitcast.247, f32[16,16,4096]{2,1,0:T(8,128)} %bitcast.235), kind=kLoop, calls=%fused_computation.69 | loop fusion | flops 16777216 | bytes 71319552 | tf_op jit(solution)/shard_map/mul | solution.py:184
  307.2 22.9 %multiply_exponential_fusion = f32[16,16,16,4096]{3,2,1,0:T(8,128)} fusion(f32[16,4096]{1,0:T(8,128)S(1)} %copy-done.16, f32[16,16,4096]{2,1,0:T(8,128)} %bitcast.234), kind=kLoop, calls=%fused_computation.68 | loop fusion | flops 16777216 | bytes 71565312 | tf_op jit(solution)/shard_map/exp | solution.py:183
  335.8 1684.3 %while.27 = (s32[]{:T(128)}, f32[16,4096]{1,0:T(8,128)}, f32[16,16,4096]{2,1,0:T(8,128)}, f32[16,16,16,4096]{3,2,1,0:T(8,128)}, f32[16,16,16,4096]{3,2,1,0:T(8,1...) while((s32[]{:T(128)}, f32[16,4096]{1,0:T(8,128)}, f32[16,16,4096]{2,1,0:T(8,128)}, ...), condition=%wide.region_16.17_spmd, body=%wide.region_14.16_spmd.sunk | while | flops 16449538 | bytes 230165872 | solution.py:198
  431.4 8.3 multiply_reduce_fusion.2
  536.6 8.3 multiply_reduce_fusion.2
  641.9 8.3 multiply_reduce_fusion.2
  747.2 8.3 multiply_reduce_fusion.2
  852.5 8.3 multiply_reduce_fusion.2
  957.7 8.3 multiply_reduce_fusion.2
  1063.0 8.3 multiply_reduce_fusion.2
  1168.3 8.3 multiply_reduce_fusion.2
  1273.5 8.3 multiply_reduce_fusion.2
  1378.8 8.3 multiply_reduce_fusion.2
  1484.0 8.3 multiply_reduce_fusion.2
  1589.3 8.3 multiply_reduce_fusion.2
  1694.6 8.3 multiply_reduce_fusion.2
  1799.8 8.3 multiply_reduce_fusion.2
  2020.2 11.4 fusion.37
  (1037 shorter events, 1680.7 us)
Async XLA Ops:
  7.2 113.4 %copy-start = (bf16[4096,32]{0,1:T(8,128)(2,1)S(1)}, bf16[4096,32]{0,1:T(8,128)(2,1)}, u32[]{:S(2)}) copy-start(bf16[4096,32]{0,1:T(8,128)(2,1)} %param.37) | copy-start | bytes 786436
  7.2 85.9 %all-gather.3.cloned.1.call-start = ((), (), s32[]{:S(2)}) async-start(), calls=%async_computation.4 | async-start | bytes 5242880 | tf_op jit(solution)/shard_map/all_gather | solution.py:75
  9.0 131.0 %all-reduce.18.cloned.1.call-start = ((), (), s32[]{:S(2)}) async-start(), calls=%async_computation.6 | async-start | bytes 524288 | tf_op jit(solution)/shard_map/psum | solution.py:170
  17.1 205.6 %all-gather.5.cloned.1.call-start = ((), (), s32[]{:S(2)}) async-start(), calls=%async_computation.5 | async-start | bytes 5242880 | tf_op jit(solution)/shard_map/all_gather | solution.py:113
  112.1 26.3 %copy-start.41 = (s32[1,16,1]{1,2,0:T(1,128)S(1)}, s32[1,16,1]{1,2,0:T(1,128)}, u32[]{:S(2)}) copy-start(s32[1,16,1]{1,2,0:T(1,128)} %param.29) | copy-start | bytes 196
  114.6 24.6 %copy-start.22 = (f32[16,4096]{1,0:T(8,128)S(1)}, f32[16,4096]{1,0:T(8,128)}, u32[]{:S(2)}) copy-start(f32[16,4096]{1,0:T(8,128)} %param.40) | copy-start | bytes 786436
  114.6 26.5 %copy-start.39 = (f32[4096]{0:T(1024)S(1)}, f32[4096]{0:T(1024)}, u32[]{:S(2)}) copy-start(f32[4096]{0:T(1024)} %param.39) | copy-start | bytes 49156
  141.1 9.2 copy-start.38
  158.2 117.6 %all-to-all-start.3 = ((bf16[4,8,8192]{2,1,0:T(8,128)(2,1)}), bf16[4,8,8192]{2,1,0:T(8,128)(2,1)S(1)}, u32[]{:S(2)}, u32[]{:S(2)}) async-start(bf16[4,8,8192]{2,1,0:T(8,128)(2,1)} %convolution_convert_fusion), calls=%async_computation.3 | async-start | bytes 1048576 | tf_op jit(solution)/shard_map/all_to_all | solution.py:98
  275.8 26.1 %copy-start.14 = (bf16[4,8,8192]{2,1,0:T(8,128)(2,1)}, bf16[4,8,8192]{2,1,0:T(8,128)(2,1)S(1)}, u32[]{:S(2)}) copy-start(bf16[4,8,8192]{2,1,0:T(8,128)(2,1)S(1)} %all-to-all-done.3) | copy-start | bytes 1572868
  275.8 26.1 %all-to-all-start = ((bf16[256,4,16]{0,2,1:T(8,128)(2,1)}), bf16[256,4,16]{0,2,1:T(8,128)(2,1)S(1)}, u32[]{:S(2)}, u32[]{:S(2)}) async-start(bf16[256,4,16]{0,2,1:T(8,128)(2,1)} %bitcast.25), calls=%async_computation | async-start | bytes 65536 | tf_op jit(solution)/shard_map/all_to_all | solution.py:139
  279.0 28.1 %copy-start.16 = (f32[16,4096]{1,0:T(8,128)S(1)}, f32[16,4096]{1,0:T(8,128)}, u32[]{:S(2)}) copy-start(f32[16,4096]{1,0:T(8,128)} %exponential_negate_fusion) | copy-start | bytes 786436
  301.9 28.2 %copy-start.20 = (bf16[256,4,16]{0,2,1:T(8,128)(2,1)}, bf16[256,4,16]{0,2,1:T(8,128)(2,1)S(1)}, u32[]{:S(2)}) copy-start(bf16[256,4,16]{0,2,1:T(8,128)(2,1)S(1)} %all-to-all-done) | copy-start | bytes 98308
  301.9 28.2 %all-to-all-start.2 = ((bf16[256,4,16]{0,2,1:T(8,128)(2,1)}), bf16[256,4,16]{0,2,1:T(8,128)(2,1)S(1)}, u32[]{:S(2)}, u32[]{:S(2)}) async-start(bf16[256,4,16]{0,2,1:T(8,128)(2,1)} %bitcast.37), calls=%async_computation.2 | async-start | bytes 65536 | tf_op jit(solution)/shard_map/all_to_all | solution.py:142
  330.6 1707.0 %all-to-all-start.1 = ((bf16[256,4,2048]{0,2,1:T(8,128)(2,1)}), bf16[256,4,2048]{0,2,1:T(8,128)(2,1)}, u32[]{:S(2)}, u32[]{:S(2)}) async-start(bf16[256,4,2048]{0,2,1:T(8,128)(2,1)} %bitcast.236), calls=%async_computation.1 | async-start | bytes 8388608 | tf_op jit(solution)/shard_map/all_to_all | solution.py:136
  335.7 1684.4 %copy-start.24 = (f32[1,4096]{1,0:T(1,128)S(1)}, f32[1,4096]{1,0:T(1,128)}, u32[]{:S(2)}) copy-start(f32[1,4096]{1,0:T(1,128)} %copy-done.23) | copy-start | bytes 49156
  335.7 1684.4 %copy-start.26 = (f32[1,4096]{1,0:T(1,128)S(1)}, f32[1,4096]{1,0:T(1,128)}, u32[]{:S(2)}) copy-start(f32[1,4096]{1,0:T(1,128)} %copy-done.25) | copy-start | bytes 49156
  335.7 1684.4 %copy-start.28 = (f32[1,4096]{1,0:T(1,128)S(1)}, f32[1,4096]{1,0:T(1,128)}, u32[]{:S(2)}) copy-start(f32[1,4096]{1,0:T(1,128)} %copy-done.27) | copy-start | bytes 49156
  335.7 1684.4 %copy-start.30 = (f32[1,4096]{1,0:T(1,128)S(1)}, f32[1,4096]{1,0:T(1,128)}, u32[]{:S(2)}) copy-start(f32[1,4096]{1,0:T(1,128)} %copy-done.29) | copy-start | bytes 49156
  335.8 1684.4 %copy-start.35 = (f32[4096]{0:T(1024)S(1)}, f32[4096]{0:T(1024)}, u32[]{:S(2)}) copy-start(f32[4096]{0:T(1024)} %param.35) | copy-start | bytes 49156
  335.8 1684.4 %copy-start.36 = (f32[4096]{0:T(1024)S(1)}, f32[4096]{0:T(1024)}, u32[]{:S(2)}) copy-start(f32[4096]{0:T(1024)} %param.41) | copy-start | bytes 49156
  2020.2 11.4 copy-start.13
  2020.2 11.7 copy-start.17
  2020.2 11.7 copy-start.19
  (145 other events, 452.4 us)
Sparse Core Ops, SparseCore 0:
  9.6 83.4 all-gather.2
  95.4 33.9 all-reduce.17
  131.1 91.5 all-gather.4
where the time goes:
time: 2080 us; the launch traced here: 2050 us
  local copies, waits for them, and re-layouts  1080 us (52%)
  other arithmetic  714 us (34%)
  waiting for transfers between devices  137 us (7%)
  matrix products  69.2 us (3%)
    pad x192, local copies, waits for them, and re-layouts, scan_block(): lax.associative_scan(combine, (decay_block, push_block), axis=0)  810 us
    add x96, other arithmetic, scan_block(): lax.associative_scan(combine, (decay_block, push_block), axis=0)  194 us
    mul x80, other arithmetic, combine(): return (former[0] * latter[0], latter[0] * former[1] + latter[1])  159 us
    concatenate x96, other arithmetic, scan_block(): lax.associative_scan(combine, (decay_block, push_block), axis=0)  139 us
    reduce_sum x16, other arithmetic, scan_block(): return (states[-1], jnp.sum(read_block[:, :, None] * states, axis=1))  133 us
    while x256, local copies, waits for them, and re-layouts  84 us
    all_gather x1, waiting for transfers between devices, body(): piece = lax.all_gather(x_attn, 'tp', axis=1, tiled=True)  76 us
    squeeze x16, local copies, waits for them, and re-layouts, body(): lax.scan(scan_block, state_prev[0], (decay.reshape(block_count, block_len...  64.1 us
  transfers between devices with their start and end apart: 7, of which 2 were waited for; matrix products, arithmetic and copies ran while one was open for 86% of the time, Pallas kernels for 0%

commit v1 on v0

v1 whole, which is shorter than its diff:
```python
import functools
import math

import jax
import jax.numpy as jnp
from jax import lax
from jax.experimental import pallas as pl
from jax.experimental.pallas import tpu as pltpu
from jax.sharding import PartitionSpec as P

HEADS = 64
KV_HEADS = 8
HEAD_DIM = 128
PAGE = 16
MASKED = -1e30
LOG2E = math.log2(math.e)
MIB = 1024 * 1024


def token_usable(page_map, slot_ids, length):
    logical = jnp.sum(
        jnp.where(
            page_map[None, :] == slot_ids[:, None], jnp.arange(page_map.shape[0])[None, :], 0
        ),
        axis=1,
    )
    positions = logical[:, None] * PAGE + jnp.arange(PAGE)[None, :]
    return (positions < length).reshape(-1)


def attention_kernel(chunk, bias_ref, query_ref, cached_ref, fresh_ref, out_ref):
    tokens = query_ref.shape[0]
    query = query_ref[...]
    scale = LOG2E / math.sqrt(HEAD_DIM)
    contract = (((1,), (1,)), ((), ()))

    def scored(keys):
        return lax.dot_general(query, keys, contract, preferred_element_type=jnp.float32) * scale

    rows = lax.broadcasted_iota(jnp.int32, (tokens, tokens), 0)
    cols = lax.broadcasted_iota(jnp.int32, (tokens, tokens), 1)
    near = jnp.where(rows >= cols, scored(fresh_ref[:, :HEAD_DIM]), MASKED)
    near_high = jnp.max(near, axis=1, keepdims=True)

    def mix(weights, values):
        return jnp.dot(
            weights.astype(jnp.bfloat16), values, preferred_element_type=jnp.float32
        )

    chunks = cached_ref.shape[0] // chunk
    if chunks == 1:
        far = scored(cached_ref[:, :HEAD_DIM]) + bias_ref[...]
        high = jnp.maximum(near_high, jnp.max(far, axis=1, keepdims=True))
        near_w = jnp.exp2(near - high)
        far_w = jnp.exp2(far - high)
        total = jnp.sum(near_w, axis=1, keepdims=True) + jnp.sum(far_w, axis=1, keepdims=True)
        mixture = mix(near_w, fresh_ref[:, HEAD_DIM:]) + mix(far_w, cached_ref[:, HEAD_DIM:])
        out_ref[...] = (mixture / total).astype(out_ref.dtype)
        return
    near_w = jnp.exp2(near - near_high)
    start = (
        near_high,
        jnp.sum(near_w, axis=1, keepdims=True),
        mix(near_w, fresh_ref[:, HEAD_DIM:]),
    )

    def step(i, carry):
        high, total, mixture = carry
        here = pl.ds(pl.multiple_of(i * chunk, chunk), chunk)
        far = scored(cached_ref[here, :HEAD_DIM]) + bias_ref[:, here]
        peak = jnp.maximum(high, jnp.max(far, axis=1, keepdims=True))
        far_w = jnp.exp2(far - peak)
        shrink = jnp.exp2(high - peak)
        return (
            peak,
            total * shrink + jnp.sum(far_w, axis=1, keepdims=True),
            mixture * shrink + mix(far_w, cached_ref[here, HEAD_DIM:]),
        )

    _, total, mixture = lax.fori_loop(0, chunks, step, start)
    out_ref[...] = (mixture / total).astype(out_ref.dtype)


def attend(queries, cached, fresh, bias, own_groups, per_group):
    tokens = queries.shape[0]
    length = cached.shape[0]
    chunk = min(1024, length)
    return pl.pallas_call(
        functools.partial(attention_kernel, chunk),
        grid=(own_groups, per_group),
        out_shape=jax.ShapeDtypeStruct(queries.shape, jnp.bfloat16),
        in_specs=[
            pl.BlockSpec((1, length), lambda g, h: (0, 0)),
            pl.BlockSpec((tokens, HEAD_DIM), lambda g, h: (0, g * per_group + h)),
            pl.BlockSpec((length, 2 * HEAD_DIM), lambda g, h: (0, g)),
            pl.BlockSpec((tokens, 2 * HEAD_DIM), lambda g, h: (0, g)),
        ],
        out_specs=pl.BlockSpec((tokens, HEAD_DIM), lambda g, h: (0, g * per_group + h)),
        compiler_params=pltpu.CompilerParams(vmem_limit_bytes=40 * MIB),
        cost_estimate=pl.CostEstimate(
            flops=4 * tokens * queries.shape[1] * (length + tokens),
            bytes_accessed=4 * queries.size + 2 * cached.size,
            transcendentals=tokens * own_groups * per_group * (length + tokens),
        ),
    )(bias, queries, cached, fresh)


def scan_kernel(
    norm_ref, spread_ref, wdt_ref, bias_ref, xconv_ref, gate_ref, alog_ref, skip_ref, init_ref,
    out_ref, final_ref, step_s, push_s, read_s,
):
    tokens, width = xconv_ref.shape
    states = alog_ref.shape[0]
    raw = jnp.dot(norm_ref[...], wdt_ref[...], preferred_element_type=jnp.float32) + bias_ref[...]
    step_size = jnp.maximum(raw, 0.0) + jnp.log1p(jnp.exp(-jnp.abs(raw)))
    step_s[...] = step_size
    push_s[...] = step_size * xconv_ref[...].astype(jnp.float32)
    rate = jnp.exp(alog_ref[...]) * (-LOG2E)
    unroll = 8

    def some(block, state):
        base = pl.multiple_of(block * unroll, unroll)
        for i in range(unroll):
            here = pl.ds(base + i, 1)
            step_row = jnp.broadcast_to(step_s[here, :], (states, width))
            push_row = jnp.broadcast_to(push_s[here, :], (states, width))
            columns = spread_ref[base + i]
            into = jnp.concatenate([columns[:states]] * (width // 128), axis=1)
            outof = jnp.concatenate([columns[states:]] * (width // 128), axis=1)
            state = jnp.exp2(step_row * rate) * state + push_row * into
            read_s[here, :] = jnp.sum(outof * state, axis=0, keepdims=True)
        return state

    final_ref[...] = lax.fori_loop(0, tokens // unroll, some, init_ref[...])
    readout = read_s[...] + skip_ref[...] * xconv_ref[...].astype(jnp.float32)
    gate = gate_ref[...].astype(jnp.float32)
    out_ref[...] = (readout * (gate * jax.nn.sigmoid(gate))).astype(out_ref.dtype)


def scan(low_norm, selection, w_dt, dt_bias, xconv, gate, a_log, d_skip, initial):
    tokens, channels = xconv.shape
    rank = low_norm.shape[1]
    states = a_log.shape[0]
    width = min(512, channels)
    spread = jnp.broadcast_to(selection[:, :, None], (tokens, 2 * states, 128))

    def whole(shape):
        return pl.BlockSpec(shape, lambda c: (0,) * len(shape))

    def columns(rows):
        return pl.BlockSpec((rows, width), lambda c: (0, c))

    return pl.pallas_call(
        scan_kernel,
        grid=(channels // width,),
        out_shape=(
            jax.ShapeDtypeStruct((tokens, channels), jnp.bfloat16),
            jax.ShapeDtypeStruct((states, channels), jnp.float32),
        ),
        in_specs=[
            whole((tokens, rank)),
            whole((tokens, 2 * states, 128)),
            columns(rank),
            columns(1),
            columns(tokens),
            columns(tokens),
            columns(states),
            columns(1),
            columns(states),
        ],
        out_specs=(columns(tokens), columns(states)),
        scratch_shapes=[pltpu.VMEM((tokens, width), jnp.float32)] * 3,
        compiler_params=pltpu.CompilerParams(vmem_limit_bytes=40 * MIB),
        cost_estimate=pl.CostEstimate(
            flops=2 * tokens * channels * rank + 7 * tokens * channels * states,
            bytes_accessed=6 * tokens * channels + 2 * rank * channels + 12 * states * channels,
            transcendentals=tokens * channels * states,
        ),
    )(
        low_norm, spread, w_dt, dt_bias[None, :], xconv, gate, a_log, d_skip[None, :], initial
    )


def body(
    x_attn,
    w_query,
    w_keyval,
    cache_pool,
    page_table,
    cached_len,
    page_dest,
    mamba_in,
    gate_in,
    conv_prev,
    state_prev,
    conv_weight,
    conv_bias,
    w_xdt,
    w_bc,
    w_dt,
    dt_bias,
    a_log,
    d_skip,
):
    tp_size = lax.axis_size("tp")
    tp_index = lax.axis_index("tp")
    token_count = x_attn.shape[0]
    own_heads = w_query.shape[1] // HEAD_DIM
    group_size = HEADS // KV_HEADS
    own_groups = max(1, own_heads // group_size)
    per_group = own_heads // own_groups
    head_cols = 2 * HEAD_DIM
    kv_cols = w_keyval.shape[1]
    slice_cols = kv_cols // tp_size
    first_group = tp_index * own_heads // group_size

    extended = jnp.concatenate([conv_prev[0], mamba_in], axis=0).astype(jnp.float32)
    convolved = jnp.broadcast_to(conv_bias[None, :], mamba_in.shape)
    for offset in range(conv_weight.shape[0]):
        convolved = (
            convolved + conv_weight[offset][None, :] * extended[offset : offset + token_count]
        )
    xconv = jax.nn.silu(convolved).astype(jnp.bfloat16)
    proj_part = jnp.dot(xconv, w_xdt, preferred_element_type=jnp.float32)
    select_part = jnp.dot(xconv, w_bc, preferred_element_type=jnp.float32)
    rank = w_xdt.shape[1]
    summed = lax.psum(
        jnp.concatenate([proj_part, select_part], axis=1).astype(jnp.bfloat16), "tp"
    ).astype(jnp.float32)
    projected, selection = summed[:, :rank], summed[:, rank:]

    local_slots = cache_pool.shape[1]
    pool = cache_pool[0].reshape(local_slots * PAGE, KV_HEADS, head_cols)
    if own_heads >= group_size:
        outgoing_kv = pool.reshape(local_slots * PAGE, tp_size, own_groups * head_cols)
    else:
        outgoing_kv = jnp.repeat(pool, group_size // own_heads, axis=1)
    outgoing_kv = jnp.moveaxis(outgoing_kv, 1, 0)
    cached = lax.all_to_all(outgoing_kv, "tp", split_axis=0, concat_axis=0, tiled=True)
    cached = cached.reshape(tp_size * local_slots * PAGE, own_groups * head_cols)
    usable = token_usable(page_table[0], jnp.arange(page_table.shape[1]), cached_len[0])
    bias = jnp.where(usable, 0.0, MASKED).astype(jnp.float32)[None, :]

    w_own = lax.dynamic_slice_in_dim(w_keyval, first_group * head_cols, own_groups * head_cols, 1)
    piece = lax.all_gather(x_attn, "tp", axis=1, tiled=True)
    low_norm = (
        projected * lax.rsqrt(jnp.mean(projected * projected, axis=-1, keepdims=True) + 1e-06)
    ).astype(jnp.bfloat16)
    mamba_out, last_state = scan(
        low_norm, selection, w_dt, dt_bias, xconv, gate_in, a_log, d_skip, state_prev[0]
    )

    fresh = jnp.dot(piece, w_own, preferred_element_type=jnp.float32).astype(jnp.bfloat16)
    queries = jnp.dot(piece, w_query, preferred_element_type=jnp.float32).astype(jnp.bfloat16)

    page_count = token_count // PAGE
    capacity = max(2, 2 * page_count // tp_size)
    target = page_dest[0, :, 0]
    page_ids = jnp.arange(page_count)
    earlier = (target[None, :] == target[:, None]) & (page_ids[None, :] < page_ids[:, None])
    ranking = jnp.sum(earlier.astype(jnp.int32), axis=1)
    slot_ids = jnp.arange(capacity)
    my_slice = lax.dynamic_slice_in_dim(
        fresh, tp_index * slice_cols - first_group * head_cols, slice_cols, 1
    )
    pieces_out = my_slice.reshape(page_count, PAGE * slice_cols)
    onehot = (
        (target[None, None, :] == jnp.arange(tp_size)[:, None, None])
        & (ranking[None, None, :] == slot_ids[None, :, None])
    ).astype(jnp.bfloat16)
    outgoing = jnp.einsum(
        "drj,jx->drx", onehot, pieces_out, preferred_element_type=jnp.float32
    ).astype(jnp.bfloat16)
    arrived = lax.all_to_all(outgoing, "tp", split_axis=0, concat_axis=2, tiled=True)
    decode = (
        arrived.reshape(capacity, tp_size, PAGE, slice_cols)
        .transpose(0, 2, 1, 3)
        .reshape(1, capacity, PAGE, kv_cols)
    )
    attn_out = attend(queries, cached, fresh, bias, own_groups, per_group)
    return (attn_out, decode, mamba_out, last_state[None])


def solution(mesh):
    return jax.shard_map(
        body,
        mesh=mesh,
        in_specs=(
            P(("grp", "pd"), "tp"),
            P(None, "tp"),
            P(),
            P(("grp", "pd"), "tp", None, None),
            P(("grp", "pd"), None),
            P(("grp", "pd")),
            P(("grp", "pd"), None, None),
            P(("grp", "pd"), "tp"),
            P(("grp", "pd"), "tp"),
            P(("grp", "pd"), None, "tp"),
            P(("grp", "pd"), None, "tp"),
            P(None, "tp"),
            P("tp"),
            P("tp", None),
            P("tp", None),
            P(None, "tp"),
            P("tp"),
            P(None, "tp"),
            P("tp"),
        ),
        out_specs=(
            P(("grp", "pd"), "tp"),
            P(("grp", "pd"), "tp", None, None),
            P(("grp", "pd"), "tp"),
            P(("grp", "pd"), None, "tp"),
        ),
        check_vma=False,
    )
```

time: 2080 us -> 199 us (0.10); the launches traced: 2050 us -> 198 us
  local copies, waits for them, and re-layouts: 1080 us -> 8.2 us
  other arithmetic: 714 us -> 7.79 us
  waiting for transfers between devices: 137 us -> 79 us
  Pallas kernels: 0 us -> 49.8 us
  matrix products: 69.2 us -> 28.5 us
    pad x192 -> x0, local copies, waits for them, and re-layouts: 810 us -> none  [scan_block(): lax.associative_scan(combine, (decay_block, push_block), axis=0)]
    add x98 -> x0, other arithmetic: 194 us -> none  [the longest x96 194 us: scan_block(): lax.associative_scan(combine, (decay_block, push_block), axis=0)]
    mul x81 -> x0, other arithmetic: 181 us -> none  [the longest x80 159 us: combine(): return (former[0] * latter[0], latter[0] * former[1] + latter[1])]
    reduce_sum x27 -> x0, other arithmetic: 142 us -> none  [the longest x16 133 us: scan_block(): return (states[-1], jnp.sum(read_block[:, :, None] * states, axis=1))]
    concatenate x96 -> x1, other arithmetic: 139 us -> 0.76 us  [body(): jnp.concatenate([proj_part, select_part], axis=1).astype(jnp.bfloat16)]
    while x257 -> x0, local copies, waits for them, and re-layouts: 84.7 us -> none
    squeeze x32 -> x0, local copies, waits for them, and re-layouts: 75.6 us -> none  [the longest x16 64.1 us: body(): lax.scan(scan_block, state_prev[0], (decay.reshape(block_count, block_len...]
    all_gather x1 -> x0, waiting for transfers between devices: 61 us -> none  [body(): everyone = lax.all_gather(queries, 'tp', axis=1, tiled=True)]
  transfers between devices with their start and end apart: 7 -> 4, of which waited for: 2 -> 2; matrix products, arithmetic and copies ran while one was open for 86% -> 16% of each run, Pallas kernels for 0% -> 25%
where the time goes in v1:
time: 199 us; the launch traced here: 198 us
  waiting for transfers between devices  79 us (40%)
  Pallas kernels  49.8 us (25%)
  matrix products  28.5 us (14%)
  between operations  14.9 us (7%)
  starting transfers between devices  10.2 us (5%)
  local copies, waits for them, and re-layouts  8.2 us (4%)
  other arithmetic  7.79 us (4%)
    all_gather x1, waiting for transfers between devices, body(): piece = lax.all_gather(x_attn, 'tp', axis=1, tiled=True)  41.5 us
    psum x1, waiting for transfers between devices, body(): lax.psum(jnp.concatenate([proj_part, select_part], axis=1).astype(jnp.bfl...  36.8 us
    pallas_call x1, Pallas kernels, scan(): pl.pallas_call(scan_kernel, grid=(channels // width,), out_shape=(jax.Sha...  35.1 us
    dot_general x1, matrix products, body(): jnp.dot(piece, w_query, preferred_element_type=jnp.float32)  16.3 us
    pallas_call x1, Pallas kernels, attend(): pl.pallas_call(functools.partial(attention_kernel, chunk), grid=(own_grou...  14.8 us
    dot_general x1, matrix products, body(): jnp.dot(piece, w_own, preferred_element_type=jnp.float32)  6.97 us
    all_to_all x1, starting transfers between devices, body(): lax.all_to_all(outgoing_kv, 'tp', split_axis=0, concat_axis=0, tiled=True)  6.45 us
  transfers between devices with their start and end apart: 4, of which 2 were waited for; matrix products, arithmetic and copies ran while one was open for 16% of the time, Pallas kernels for 25%

profile of v1, /device:TPU:0, one launch (start us, length us, event | category | flops | bytes accessed | tf_op | source)
XLA Modules:
  0.0 198.4 jit_solution(16841734106529385437)
XLA Ops:
  7.2 1.1 fusion.18
  8.3 2.2 %maximum_convert_fusion = f32[259,4096]{1,0:T(8,128)S(1)} fusion(bf16[256,4096]{1,0:T(8,128)(2,1)} %param.26, bf16[3,4096]{1,0:T(4,128)(2,1)} %bitcast.46), kind=kLoop, calls=%fused_computation.13 | loop fusion | flops 4243456 | bytes 6365184 | tf_op jit(solution)/shard_map/convert_element_type | solution.py:217
  10.5 2.7 %multiply_convert_fusion.xconv_ref = bf16[256,4096]{1,0:T(8,128)(2,1)S(1)} fusion(f32[259,4096]{1,0:T(8,128)S(1)} %maximum_convert_fusion, f32[4096]{0:T(1024)S(1)} %bitcast.44, f32[4096]{0:T(1024)S(1)} %bitcast.45, f32[4096]{0:T(1024)S(1)} %bitcast.43, f32[4096]{0:T(1024)S(1)} %bitcast.42, f32[4096]{0:T(1024)S(1)} %copy-done.8), kind=kLoop, calls=%fused_computation.11 | loop fusion | flops 13631488 | bytes 18956288 | tf_op jit(solution)/shard_map/convert_element_type | solution.py:223
  13.2 0.7 convolution_convert_fusion.3
  14.1 3.4 %convolution_convert_fusion.2 = bf16[256,512]{1,0:T(8,128)(2,1)S(1)} fusion(bf16[256,4096]{1,0:T(8,128)(2,1)S(1)} %multiply_convert_fusion.xconv_ref, bf16[4096,512]{1,0:T(8,128)(2,1)} %param.32), kind=kOutput, calls=%fused_computation.14 | convolution fusion | flops 1073872896 | bytes 6553600 | tf_op jit(solution)/shard_map/dot_general | solution.py:224
  17.6 0.8 pad_maximum_fusion
  18.4 0.7 all-gather.2.cloned.1.call-update
  19.1 1.8 reshape_reshape_squeeze.3
  21.0 1.2 copy.41
  22.1 6.4 %all-to-all-start = ((bf16[4,256,512]{2,1,0:T(8,128)(2,1)}), bf16[4,256,512]{2,1,0:T(8,128)(2,1)S(1)}, u32[]{:S(2)}, u32[]{:S(2)}) async-start(bf16[4,256,512]{2,1,0:T(8,128)(2,1)} %bitcast.40), calls=%async_computation | async-start | bytes 2097152 | tf_op jit(solution)/shard_map/all_to_all | solution.py:239
  29.5 0.2 convert_reduce_fusion
  29.7 36.8 %all-reduce.2.cloned.1.call-done = bf16[256,544]{1,0:T(8,128)(2,1)} async-done(((bf16[256,544]{1,0:T(8,128)(2,1)}), bf16[256,544]{1,0:T(8,128)(2,1)}) %all-reduce.2.cloned.1.call-update) | async-done | bytes 278544 | tf_op jit(solution)/shard_map/psum | solution.py:227
  66.5 1.0 slice.45
  67.5 1.5 convert_element_type.35
  69.3 1.1 broadcast_in_dim.57.spread_ref
  70.5 35.1 %shard_map.211 = (bf16[256,4096]{1,0:T(8,128)(2,1)}, f32[16,4096]{1,0:T(8,128)}) custom-call(bf16[256,512]{1,0:T(8,128)(2,1)S(1)} %multiply_convert_fusion.1.norm_ref, f32[256,32,128]{2,1,0:T(8,128)S(1)} %broadcast_in_dim.57.spread_ref, bf16[512,4096]{1,0:T(8,128)(2,1)S(1)} %copy-done.2, f32[1,4096]{1,0:T(1,128)S(1)} %bitcast.38, ...), custom_call_target="tpu_custom_call" | custom-call | flops 1191182336 | bytes 11272192 | tf_op jit(solution)/shard_map/pallas_call | solution.py:153
  105.5 41.5 %all-gather.2.cloned.1.call-done = bf16[256,8192]{1,0:T(8,128)(2,1)} async-done(((bf16[256,2048]{1,0:T(8,128)(2,1)}), bf16[256,8192]{1,0:T(8,128)(2,1)}) %all-gather.2.cloned.1.call-update) | async-done | bytes 4194320 | tf_op jit(solution)/shard_map/all_gather | solution.py:245
  147.0 7.0 %fusion.9.fresh_ref = bf16[256,512]{1,0:T(8,128)(2,1)S(1)} fusion(bf16[256,8192]{1,0:T(8,128)(2,1)} %all-gather.2.cloned.1.call-done, bf16[8192,2048]{1,0:T(8,128)(2,1)} %param.21, s32[]{:T(128)S(6)} %select_n.31), kind=kOutput, calls=%fused_computation.16 | convolution fusion | flops 2147614720 | bytes 12845060 | tf_op jit(solution)/shard_map/dot_general | solution.py:253
  154.2 1.1 convolution_convert_fusion
  155.2 3.7 %all-to-all-start.1 = ((bf16[4,8,8192]{2,1,0:T(8,128)(2,1)}), bf16[4,8,8192]{2,1,0:T(8,128)(2,1)S(1)}, u32[]{:S(2)}, u32[]{:S(2)}) async-start(bf16[4,8,8192]{2,1,0:T(8,128)(2,1)} %convolution_convert_fusion), calls=%async_computation.1 | async-start | bytes 1048576 | tf_op jit(solution)/shard_map/all_to_all | solution.py:274
  158.9 16.3 %convolution_convert_fusion.1.query_ref = bf16[256,2048]{1,0:T(8,128)(2,1)S(1)} fusion(bf16[256,8192]{1,0:T(8,128)(2,1)} %all-gather.2.cloned.1.call-done, bf16[8192,2048]{1,0:T(8,128)(2,1)} %param.20), kind=kOutput, calls=%fused_computation.12 | convolution fusion | flops 8590458880 | bytes 38797312 | tf_op jit(solution)/shard_map/dot_general | solution.py:254
  175.2 14.8 %shard_map.210 = bf16[256,2048]{1,0:T(8,128)(2,1)} custom-call(f32[1,1024]{1,0:T(1,128)S(1)} %select_n.29.bias_ref, bf16[256,2048]{1,0:T(8,128)(2,1)S(1)} %convolution_convert_fusion.1.query_ref, bf16[1024,512]{1,0:T(8,128)(2,1)S(1)} %bitcast.36, bf16[256,512]{1,0:T(8,128)(2,1)S(1)} %fusion.9.fresh_ref), custom_call_target="tpu_custom_call" | custom-call | flops 2684354560 | bytes 3145728 | tf_op jit(solution)/shard_map/pallas_call | solution.py:88
  189.9 0.4 copy.37
  190.4 1.2 reshape.121
  (38 shorter events, 0.9 us)
Async XLA Ops:
  7.2 6.1 %copy-start = (bf16[4096,32]{0,1:T(8,128)(2,1)S(1)}, bf16[4096,32]{0,1:T(8,128)(2,1)}, u32[]{:S(2)}) copy-start(bf16[4096,32]{0,1:T(8,128)(2,1)} %param.33) | copy-start | bytes 786436
  7.2 3.3 %copy-start.8 = (f32[4096]{0:T(1024)S(1)}, f32[4096]{0:T(1024)}, u32[]{:S(2)}) copy-start(f32[4096]{0:T(1024)} %param.31) | copy-start | bytes 49156
  7.2 59.3 %all-reduce.2.cloned.1.call-start = ((), (), s32[]{:S(2)}) async-start(), calls=%async_computation.3 | async-start | bytes 655360 | tf_op jit(solution)/shard_map/psum | solution.py:227
  17.6 11.7 %copy-start.9 = (s32[1,64]{1,0:T(1,128)S(1)}, s32[1,64]{1,0:T(1,128)}, u32[]{:S(2)}) copy-start(s32[1,64]{1,0:T(1,128)} %param.23) | copy-start | bytes 772
  17.6 12.0 %copy-start.10 = (s32[1,16,1]{1,2,0:T(1,128)S(1)}, s32[1,16,1]{1,2,0:T(1,128)}, u32[]{:S(2)}) copy-start(s32[1,16,1]{1,2,0:T(1,128)} %param.25) | copy-start | bytes 196
  18.4 128.7 %all-gather.2.cloned.1.call-start = ((), (), s32[]{:S(2)}) async-start(), calls=%async_computation.2 | async-start | bytes 5242880 | tf_op jit(solution)/shard_map/all_gather | solution.py:245
  22.1 48.3 %copy-start.4 = (f32[16,4096]{1,0:T(8,128)S(1)}, f32[16,4096]{1,0:T(8,128)}, u32[]{:S(2)}) copy-start(f32[16,4096]{1,0:T(8,128)} %alog_ref.1) | copy-start | bytes 786436
  22.1 48.3 %copy-start.6 = (f32[4096]{0:T(1024)S(1)}, f32[4096]{0:T(1024)}, u32[]{:S(2)}) copy-start(f32[4096]{0:T(1024)} %param.35) | copy-start | bytes 49156
  22.1 48.3 %copy-start.7 = (f32[4096]{0:T(1024)S(1)}, f32[4096]{0:T(1024)}, u32[]{:S(2)}) copy-start(f32[4096]{0:T(1024)} %param.37) | copy-start | bytes 49156
  22.1 133.1 %all-to-all-start = ((bf16[4,256,512]{2,1,0:T(8,128)(2,1)}), bf16[4,256,512]{2,1,0:T(8,128)(2,1)S(1)}, u32[]{:S(2)}, u32[]{:S(2)}) async-start(bf16[4,256,512]{2,1,0:T(8,128)(2,1)} %bitcast.40), calls=%async_computation | async-start | bytes 2097152 | tf_op jit(solution)/shard_map/all_to_all | solution.py:239
  66.5 3.9 %copy-start.2 = (bf16[512,4096]{1,0:T(8,128)(2,1)S(1)}, bf16[512,4096]{1,0:T(8,128)(2,1)}, u32[]{:S(2)}) copy-start(bf16[512,4096]{1,0:T(8,128)(2,1)} %wdt_ref.1) | copy-start | bytes 12582916
  66.5 3.9 %copy-start.3 = (bf16[256,4096]{1,0:T(8,128)(2,1)S(1)}, bf16[256,4096]{1,0:T(8,128)(2,1)}, u32[]{:S(2)}) copy-start(bf16[256,4096]{1,0:T(8,128)(2,1)} %gate_ref.1) | copy-start | bytes 6291460
  66.5 4.0 %copy-start.5 = (f32[1,16,4096]{2,1,0:T(8,128)S(1)}, f32[1,16,4096]{2,1,0:T(8,128)}, u32[]{:S(2)}) copy-start(f32[1,16,4096]{2,1,0:T(8,128)} %param.29) | copy-start | bytes 786436
  155.2 34.7 %all-to-all-start.1 = ((bf16[4,8,8192]{2,1,0:T(8,128)(2,1)}), bf16[4,8,8192]{2,1,0:T(8,128)(2,1)S(1)}, u32[]{:S(2)}, u32[]{:S(2)}) async-start(bf16[4,8,8192]{2,1,0:T(8,128)(2,1)} %convolution_convert_fusion), calls=%async_computation.1 | async-start | bytes 1048576 | tf_op jit(solution)/shard_map/all_to_all | solution.py:274
  175.2 16.4 %copy-start.1 = (bf16[4096,32]{0,1:T(8,128)(2,1)S(1)}, bf16[4096,32]{0,1:T(8,128)(2,1)}, u32[]{:S(2)}) copy-start(bf16[4096,32]{0,1:T(8,128)(2,1)} %param.33) | copy-start | bytes 786436
Sparse Core Ops, SparseCore 0:
  18.5 47.9 all-reduce.1
  68.1 78.9 all-gather.1

commit v2 on v1

--- a/solution.py
+++ b/solution.py
@@ -179,6 +179,85 @@
     )(
         low_norm, spread, w_dt, dt_bias[None, :], xconv, gate, a_log, d_skip[None, :], initial
     )
+
+
+def project_kernel(count, has_sum, where_ref, *refs):
+    pieces, weight_ref = refs[:count], refs[count]
+    out_ref, total = refs[-2], refs[-1]
+    at = pl.program_id(1)
+
+    @pl.when(at == 0)
+    def _():
+        total[...] = refs[count + 1][...] if has_sum else jnp.zeros_like(total)
+
+    for i in range(count):
+
+        @pl.when(at == i)
+        def _(i=i):
+            total[...] += jnp.dot(
+                pieces[i][...], weight_ref[...], preferred_element_type=jnp.float32
+            )
+
+    @pl.when(at == count - 1)
+    def _():
+        out_ref[...] = total[...].astype(out_ref.dtype)
+
+
+def project(pieces, owners, weight, base, columns, so_far=None, dtype=jnp.bfloat16):
+    rows, depth = pieces[0].shape
+    count = len(pieces)
+    width = min(512, columns)
+    blocks = columns // width
+    where = jnp.stack([jnp.asarray(w, jnp.int32) for w in (*owners, base)])
+    in_specs = [pl.BlockSpec((rows, depth), lambda n, p, w: (0, 0))] * count
+    in_specs.append(pl.BlockSpec((depth, width), lambda n, p, w: (w[p], w[count] * blocks + n)))
+    operands = [*pieces, weight]
+    if so_far is not None:
+        in_specs.append(pl.BlockSpec((rows, width), lambda n, p, w: (0, n)))
+        operands.append(so_far)
+    return pl.pallas_call(
+        functools.partial(project_kernel, count, so_far is not None),
+        grid_spec=pltpu.PrefetchScalarGridSpec(
+            num_scalar_prefetch=1,
+            grid=(blocks, count),
+            in_specs=in_specs,
+            out_specs=pl.BlockSpec((rows, width), lambda n, p, w: (0, n)),
+            scratch_shapes=[pltpu.VMEM((rows, width), jnp.float32)],
+        ),
+        out_shape=jax.ShapeDtypeStruct((rows, columns), dtype),
+        compiler_params=pltpu.CompilerParams(vmem_limit_bytes=40 * MIB),
+        cost_estimate=pl.CostEstimate(
+            flops=2 * rows * depth * count * columns,
+            bytes_accessed=2 * depth * count * (columns + rows) + 4 * rows * columns,
+            transcendentals=0,
+        ),
+    )(where, *operands)
+
+
+def exchange_sum(part, size):
+    if size != 4:
+        return lax.psum(part, "tp").astype(jnp.float32)
+    total = part.astype(jnp.float32)
+    for shift in (1, 2, 3):
+        total = total + lax.ppermute(
+            part, "tp", [(t, (t + shift) % size) for t in range(size)]
+        ).astype(jnp.float32)
+    return total
+
+
+def relay(own, size):
+    right = left = own
+    rights, lefts = [], []
+    for step in range(1, size):
+        right = lax.ppermute(right, "tp", [(t, t + 1) for t in range(step - 1, size - 1)])
+        left = lax.ppermute(left, "tp", [(t, t - 1) for t in range(1, size - step + 1)])
+        rights.append(right)
+        lefts.append(left)
+    me = lax.axis_index("tp")
+    found = [
+        jnp.where(me >= k, rights[k - 1], lefts[size - k - 1]) for k in range(1, size)
+    ]
+    return found, rights, lefts
 
 
 def body(
@@ -214,6 +293,10 @@
     slice_cols = kv_cols // tp_size
     first_group = tp_index * own_heads // group_size
 
+    line = tp_size == 4
+    if line:
+        others, rights, lefts = relay(x_attn, tp_size)
+
     extended = jnp.concatenate([conv_prev[0], mamba_in], axis=0).astype(jnp.float32)
     convolved = jnp.broadcast_to(conv_bias[None, :], mamba_in.shape)
     for offset in range(conv_weight.shape[0]):
@@ -224,9 +307,10 @@
     proj_part = jnp.dot(xconv, w_xdt, preferred_element_type=jnp.float32)
     select_part = jnp.dot(xconv, w_bc, preferred_element_type=jnp.float32)
     rank = w_xdt.shape[1]
-    summed = lax.psum(
-        jnp.concatenate([proj_part, select_part], axis=1).astype(jnp.bfloat16), "tp"
-    ).astype(jnp.float32)
+    parts = jnp.concatenate([proj_part, select_part], axis=1).astype(jnp.bfloat16)
+    if line:
+        parts, _, _ = lax.optimization_barrier((parts, rights[0], lefts[0]))
+    summed = exchange_sum(parts, tp_size)
     projected, selection = summed[:, :rank], summed[:, rank:]
 
     local_slots = cache_pool.shape[1]
@@ -236,22 +320,34 @@
     else:
         outgoing_kv = jnp.repeat(pool, group_size // own_heads, axis=1)
     outgoing_kv = jnp.moveaxis(outgoing_kv, 1, 0)
+    if line:
+        outgoing_kv, _, _ = lax.optimization_barrier((outgoing_kv, rights[1], lefts[1]))
     cached = lax.all_to_all(outgoing_kv, "tp", split_axis=0, concat_axis=0, tiled=True)
     cached = cached.reshape(tp_size * local_slots * PAGE, own_groups * head_cols)
     usable = token_usable(page_table[0], jnp.arange(page_table.shape[1]), cached_len[0])
     bias = jnp.where(usable, 0.0, MASKED).astype(jnp.float32)[None, :]
 
-    w_own = lax.dynamic_slice_in_dim(w_keyval, first_group * head_cols, own_groups * head_cols, 1)
-    piece = lax.all_gather(x_attn, "tp", axis=1, tiled=True)
+    kv_own = own_groups * head_cols
+    kv_base = first_group // own_groups
+    if line:
+        fresh_sum = project([x_attn], [tp_index], w_keyval, kv_base, kv_own, None, jnp.float32)
+        query_sum = project([x_attn], [tp_index], w_query, 0, w_query.shape[1], None, jnp.float32)
+        owners = [(tp_index + tp_size - k) % tp_size for k in range(1, tp_size)]
+    else:
+        fresh_sum = query_sum = None
+        others = [lax.all_gather(x_attn, "tp", axis=1, tiled=True)]
+        owners = [0]
     low_norm = (
         projected * lax.rsqrt(jnp.mean(projected * projected, axis=-1, keepdims=True) + 1e-06)
     ).astype(jnp.bfloat16)
+    if line:
+        low_norm, _, _ = lax.optimization_barrier((low_norm, rights[1], lefts[1]))
     mamba_out, last_state = scan(
         low_norm, selection, w_dt, dt_bias, xconv, gate_in, a_log, d_skip, state_prev[0]
     )
 
-    fresh = jnp.dot(piece, w_own, preferred_element_type=jnp.float32).astype(jnp.bfloat16)
-    queries = jnp.dot(piece, w_query, preferred_element_type=jnp.float32).astype(jnp.bfloat16)
+    fresh = project(others, owners, w_keyval, kv_base, kv_own, fresh_sum)
+    queries = project(others, owners, w_query, 0, w_query.shape[1], query_sum)
 
     page_count = token_count // PAGE
     capacity = max(2, 2 * page_count // tp_size)

time: 199 us -> 189 us (0.950)
  waiting for transfers between devices: 79 us -> 40.3 us
  Pallas kernels: 49.8 us -> 81.3 us
  matrix products: 28.5 us -> 6.17 us
  starting transfers between devices: 10.2 us -> 29.9 us
  between operations: 14.9 us -> 1.78 us
  other arithmetic: 7.79 us -> 14.3 us
  local copies, waits for them, and re-layouts: 8.2 us -> 14.7 us
    all_gather x1 -> x0, waiting for transfers between devices: 41.5 us -> none  [body(): piece = lax.all_gather(x_attn, 'tp', axis=1, tiled=True)]
    ppermute x0 -> x9, waiting for transfers between devices: none -> 40.3 us  [the longest x3 27.5 us: exchange_sum(): lax.ppermute(part, 'tp', [(t, (t + shift) % size) for t in range(size)])]
    psum x1 -> x0, waiting for transfers between devices: 36.8 us -> none  [body(): lax.psum(jnp.concatenate([proj_part, select_part], axis=1).astype(jnp.bfl...]
    pallas_call x0 -> x4, Pallas kernels: none -> 30.3 us  [project(): pl.pallas_call(functools.partial(project_kernel, count, so_far is not Non...]
    dot_general x2 -> x0, matrix products: 23.2 us -> none  [the longest x1 16.3 us: body(): jnp.dot(piece, w_query, preferred_element_type=jnp.float32)]
    ppermute x0 -> x9, starting transfers between devices: none -> 18.2 us  [the longest x3 8.62 us: relay(): lax.ppermute(right, 'tp', [(t, t + 1) for t in range(step - 1, size - 1)])]
    select_n x0 -> x3, other arithmetic: none -> 4.54 us  [relay(): jnp.where(me >= k, rights[k - 1], lefts[size - k - 1])]
    unnamed x22 -> x34, local copies, waits for them, and re-layouts: 0.06 us -> 3.78 us
  transfers between devices with their start and end apart: 4 -> 11, of which waited for: 2 -> 3; matrix products, arithmetic and copies ran while one was open for 16% -> 15% of each run, Pallas kernels for 25% -> 43%
where the time goes in v2:
time: 189 us; the launch traced here: 188 us
  Pallas kernels  81.3 us (43%)
  waiting for transfers between devices  40.3 us (21%)
  starting transfers between devices  29.9 us (16%)
  local copies, waits for them, and re-layouts  14.7 us (8%)
  other arithmetic  14.3 us (8%)
  matrix products  6.17 us (3%)
    pallas_call x1, Pallas kernels, scan(): pl.pallas_call(scan_kernel, grid=(channels // width,), out_shape=(jax.Sha...  35 us
    pallas_call x4, Pallas kernels, project(): pl.pallas_call(functools.partial(project_kernel, count, so_far is not Non...  30.3 us
    ppermute x3, waiting for transfers between devices, exchange_sum(): lax.ppermute(part, 'tp', [(t, (t + shift) % size) for t in range(size)])  27.5 us
    pallas_call x1, Pallas kernels, attend(): pl.pallas_call(functools.partial(attention_kernel, chunk), grid=(own_grou...  16 us
    ppermute x3, waiting for transfers between devices, relay(): lax.ppermute(left, 'tp', [(t, t - 1) for t in range(1, size - step + 1)])  12.8 us
    ppermute x3, starting transfers between devices, relay(): lax.ppermute(right, 'tp', [(t, t + 1) for t in range(step - 1, size - 1)])  8.62 us
    all_to_all x1, starting transfers between devices, body(): lax.all_to_all(outgoing, 'tp', split_axis=0, concat_axis=2, tiled=True)  6.57 us
    ppermute x3, starting transfers between devices, exchange_sum(): lax.ppermute(part, 'tp', [(t, (t + shift) % size) for t in range(size)])  5.76 us
  transfers between devices with their start and end apart: 11, of which 3 were waited for; matrix products, arithmetic and copies ran while one was open for 15% of the time, Pallas kernels for 43%

profile of v2, /device:TPU:0, one launch (start us, length us, event | category | flops | bytes accessed | tf_op | source)
XLA Modules:
  0.0 188.4 jit_solution(10840088033639879765)
XLA Ops:
  0.7 6.0 %collective-permute-start = (bf16[256,2048]{1,0:T(8,128)(2,1)}, bf16[256,2048]{1,0:T(8,128)(2,1)}, u32[]{:S(2)}, u32[]{:S(2)}) collective-permute-start(bf16[256,2048]{1,0:T(8,128)(2,1)} %refs_0_.3), channel_id=1, source_target_pairs={{0,4},{4,8},{8,12},{1,5},{5,9},{9,13},{2,6},{6,10},{10,14},{3,7},{... | collective-permute-start | bytes 3145736 | tf_op jit(solution)/shard_map/ppermute | solution.py:252
  11.1 2.2 %maximum_convert_fusion = f32[259,4096]{1,0:T(8,128)S(1)} fusion(bf16[256,4096]{1,0:T(8,128)(2,1)} %param.26, bf16[3,4096]{1,0:T(4,128)(2,1)} %bitcast.44), kind=kLoop, calls=%fused_computation.10 | loop fusion | flops 4243456 | bytes 6365184 | tf_op jit(solution)/shard_map/convert_element_type | solution.py:300
  13.3 2.7 %multiply_convert_fusion.xconv_ref = bf16[256,4096]{1,0:T(8,128)(2,1)S(1)} fusion(f32[259,4096]{1,0:T(8,128)S(1)} %maximum_convert_fusion, f32[4096]{0:T(1024)S(1)} %bitcast.42, f32[4096]{0:T(1024)S(1)} %bitcast.43, f32[4096]{0:T(1024)S(1)} %bitcast.41, f32[4096]{0:T(1024)S(1)} %bitcast.40, f32[4096]{0:T(1024)S(1)} %copy-done.14), kind=kLoop, calls=%fused_computation.9 | loop fusion | flops 13631488 | bytes 18956288 | tf_op jit(solution)/shard_map/convert_element_type | solution.py:306
  17.3 3.4 %convolution_convert_fusion.1 = bf16[256,512]{1,0:T(8,128)(2,1)S(1)} fusion(bf16[256,4096]{1,0:T(8,128)(2,1)S(1)} %multiply_convert_fusion.xconv_ref, bf16[4096,512]{1,0:T(8,128)(2,1)} %param.32), kind=kOutput, calls=%fused_computation.11 | convolution fusion | flops 1073872896 | bytes 6553600 | tf_op jit(solution)/shard_map/dot_general | solution.py:307
  20.7 12.8 %collective-permute-done.1 = bf16[256,2048]{1,0:T(8,128)(2,1)} collective-permute-done((bf16[256,2048]{1,0:T(8,128)(2,1)}, bf16[256,2048]{1,0:T(8,128)(2,1)}, u32[]{:S(2)}, u32[]{:S(2)}) %collective-permute-start.1) | collective-permute-done | bytes 1048608 | tf_op jit(solution)/shard_map/ppermute | solution.py:253
  37.3 3.1 %collective-permute-start.7 = (bf16[256,544]{1,0:T(8,128)(2,1)}, bf16[256,544]{1,0:T(8,128)(2,1)}, u32[]{:S(2)}, u32[]{:S(2)}) collective-permute-start(bf16[256,544]{1,0:T(8,128)(2,1)} %pad_maximum_fusion), channel_id=1, source_target_pairs={{0,8},{4,12},{8,0},{12,4},{1,9},{5,13},{9,1},{13,5},{2,10},{6,14},... | collective-permute-start | bytes 835592 | tf_op jit(solution)/shard_map/ppermute | solution.py:242
  40.4 1.6 collective-permute-start.6
  42.2 2.6 %reshape_reshape_squeeze.3 = bf16[256,4,512]{2,1,0:T(4,128)(2,1)} reshape(bf16[1,16,16,2048]{3,2,1,0:T(8,128)(2,1)} %param.22) | data formatting | bytes 2097152 | tf_op jit(solution)/shard_map/reshape;reshape;squeeze | solution.py:319
  44.8 2.4 %copy.36 = bf16[256,4,512]{2,0,1:T(8,128)(2,1)} copy(bf16[256,4,512]{2,1,0:T(4,128)(2,1)} %reshape_reshape_squeeze.3) | data formatting | bytes 2097152 | tf_op jit(solution)/shard_map/reshape;reshape;squeeze | solution.py:319
  47.3 2.8 %shard_map.212.refs_4_ = f32[256,512]{1,0:T(8,128)S(1)} custom-call(s32[2]{0:T(128)S(1)} %get-tuple-element.21.where_ref, bf16[256,2048]{1,0:T(8,128)(2,1)S(1)} %copy-done.4, bf16[8192,2048]{1,0:T(8,128)(2,1)} %refs_3_.3), custom_call_target="tpu_custom_call" | custom-call | flops 536870912 | bytes 3670016 | tf_op jit(solution)/shard_map/pallas_call | solution.py:218
  50.9 1.7 collective-permute-start.4
  52.6 6.2 %shard_map.210.refs_4_ = f32[256,2048]{1,0:T(8,128)S(1)} custom-call(s32[2]{0:T(128)S(1)} %get-tuple-element.20.where_ref, bf16[256,2048]{1,0:T(8,128)(2,1)S(1)} %copy-done.4, bf16[8192,2048]{1,0:T(8,128)(2,1)} %refs_3_.2), custom_call_target="tpu_custom_call" | custom-call | flops 2147483648 | bytes 11534336 | tf_op jit(solution)/shard_map/pallas_call | solution.py:218
  60.1 13.3 %collective-permute-done.8 = bf16[256,544]{1,0:T(8,128)(2,1)} collective-permute-done((bf16[256,544]{1,0:T(8,128)(2,1)}, bf16[256,544]{1,0:T(8,128)(2,1)}, u32[]{:S(2)}, u32[]{:S(2)}) %collective-permute-start.8) | collective-permute-done | bytes 278560 | tf_op jit(solution)/shard_map/ppermute | solution.py:242
  73.5 14.1 %collective-permute-done.7 = bf16[256,544]{1,0:T(8,128)(2,1)} collective-permute-done((bf16[256,544]{1,0:T(8,128)(2,1)}, bf16[256,544]{1,0:T(8,128)(2,1)}, u32[]{:S(2)}, u32[]{:S(2)}) %collective-permute-start.7) | collective-permute-done | bytes 278560 | tf_op jit(solution)/shard_map/ppermute | solution.py:242
  90.6 5.1 %all-to-all-start = ((bf16[4,256,512]{2,1,0:T(8,128)(2,1)}), bf16[4,256,512]{2,1,0:T(8,128)(2,1)}, u32[]{:S(2)}, u32[]{:S(2)}) async-start(bf16[4,256,512]{2,1,0:T(8,128)(2,1)} %bitcast.39), calls=%async_computation | async-start | bytes 2097152 | tf_op jit(solution)/shard_map/all_to_all | solution.py:325
  96.6 1.8 broadcast_select_fusion.1.refs_1_
  99.6 35.0 %shard_map.215 = (bf16[256,4096]{1,0:T(8,128)(2,1)}, f32[16,4096]{1,0:T(8,128)}) custom-call(bf16[256,512]{1,0:T(8,128)(2,1)S(1)} %multiply_convert_fusion.1.norm_ref, f32[256,32,128]{2,1,0:T(8,128)S(1)} %broadcast_in_dim.57.spread_ref, bf16[512,4096]{1,0:T(8,128)(2,1)S(1)} %copy-done.7, f32[1,4096]{1,0:T(1,128)S(1)} %bitcast.37, ...), custom_call_target="tpu_custom_call" | custom-call | flops 1191182336 | bytes 11272192 | tf_op jit(solution)/shard_map/pallas_call | solution.py:153
  137.5 5.2 %shard_map.213.fresh_ref = bf16[256,512]{1,0:T(8,128)(2,1)S(1)} custom-call(s32[4]{0:T(128)S(1)} %get-tuple-element.14.where_ref, bf16[256,2048]{1,0:T(8,128)(2,1)S(1)} %broadcast_select_fusion.2.refs_0_, bf16[256,2048]{1,0:T(8,128)(2,1)S(1)} %broadcast_select_fusion.1.refs_1_, bf16[256,2048]{1,0:T(8,128)(2,1)S(1)} %broadcast_select_fusion.refs_2_, ...), custom_call_target="tpu_custom_call" | custom-call | flops 1610612736 | bytes 9961472 | tf_op jit(solution)/shard_map/pallas_call | solution.py:218
  143.5 2.0 %convolution_convert_fusion = bf16[4,8,8192]{2,1,0:T(8,128)(2,1)} fusion(bf16[16,8192,1]{1,0,2:T(8,128)(2,1)} %reshape.122, pred[8,16]{1,0:T(8,128)(4,1)S(1)} %iota_compare_fusion.2, pred[4,16]{1,0:T(4,128)(4,1)S(1)} %copy-done.15), kind=kOutput, calls=%fused_computation | convolution fusion | flops 8651264 | bytes 786624 | tf_op jit(solution)/shard_map/drj,jx->drx/dot_general | solution.py:367
  145.5 6.6 %all-to-all-start.1 = ((bf16[4,8,8192]{2,1,0:T(8,128)(2,1)}), bf16[4,8,8192]{2,1,0:T(8,128)(2,1)}, u32[]{:S(2)}, u32[]{:S(2)}) async-start(bf16[4,8,8192]{2,1,0:T(8,128)(2,1)} %convolution_convert_fusion), calls=%async_computation.1 | async-start | bytes 1048576 | tf_op jit(solution)/shard_map/all_to_all | solution.py:370
  152.1 1.6 copy-done.3
  153.7 16.1 %shard_map.211.query_ref = bf16[256,2048]{1,0:T(8,128)(2,1)S(1)} custom-call(s32[4]{0:T(128)S(1)} %pad_add_fusion.where_ref, bf16[256,2048]{1,0:T(8,128)(2,1)S(1)} %broadcast_select_fusion.2.refs_0_, bf16[256,2048]{1,0:T(8,128)(2,1)S(1)} %broadcast_select_fusion.1.refs_1_, bf16[256,2048]{1,0:T(8,128)(2,1)S(1)} %broadcast_select_fusion.refs_2_, ...), custom_call_target="tpu_custom_call" | custom-call | flops 6442450944 | bytes 30408704 | tf_op jit(solution)/shard_map/pallas_call | solution.py:218
  169.8 16.0 %shard_map.214 = bf16[256,2048]{1,0:T(8,128)(2,1)} custom-call(f32[1,1024]{1,0:T(1,128)S(1)} %select_n.63.bias_ref, bf16[256,2048]{1,0:T(8,128)(2,1)S(1)} %shard_map.211.query_ref, bf16[1024,512]{1,0:T(8,128)(2,1)} %bitcast.7.cached_ref, bf16[256,512]{1,0:T(8,128)(2,1)S(1)} %shard_map.213.fresh_ref), custom_call_target="tpu_custom_call" | custom-call | flops 2684354560 | bytes 3145728 | tf_op jit(solution)/shard_map/pallas_call | solution.py:88
  185.8 1.4 copy.33
  (71 shorter events, 20.7 us)
Async XLA Ops:
  0.6 15.4 %copy-start = (bf16[4096,32]{0,1:T(8,128)(2,1)S(1)}, bf16[4096,32]{0,1:T(8,128)(2,1)}, u32[]{:S(2)}) copy-start(bf16[4096,32]{0,1:T(8,128)(2,1)} %param.33) | copy-start | bytes 786436
  0.6 12.7 %copy-start.14 = (f32[4096]{0:T(1024)S(1)}, f32[4096]{0:T(1024)}, u32[]{:S(2)}) copy-start(f32[4096]{0:T(1024)} %param.31) | copy-start | bytes 49156
  0.7 35.6 %collective-permute-start = (bf16[256,2048]{1,0:T(8,128)(2,1)}, bf16[256,2048]{1,0:T(8,128)(2,1)}, u32[]{:S(2)}, u32[]{:S(2)}) collective-permute-start(bf16[256,2048]{1,0:T(8,128)(2,1)} %refs_0_.3), channel_id=1, source_target_pairs={{0,4},{4,8},{8,12},{1,5},{5,9},{9,13},{2,6},{6,10},{10,14},{3,7},{... | collective-permute-start | bytes 3145736 | tf_op jit(solution)/shard_map/ppermute | solution.py:252
  6.7 26.8 %collective-permute-start.1 = (bf16[256,2048]{1,0:T(8,128)(2,1)}, bf16[256,2048]{1,0:T(8,128)(2,1)}, u32[]{:S(2)}, u32[]{:S(2)}) collective-permute-start(bf16[256,2048]{1,0:T(8,128)(2,1)} %refs_0_.3), channel_id=1, source_target_pairs={{4,0},{8,4},{12,8},{5,1},{9,5},{13,9},{6,2},{10,6},{14,10},{7,3},{... | collective-permute-start | bytes 3145736 | tf_op jit(solution)/shard_map/ppermute | solution.py:253
  13.3 3.6 %copy-start.16 = (s32[1,16,1]{1,2,0:T(1,128)S(1)}, s32[1,16,1]{1,2,0:T(1,128)}, u32[]{:S(2)}) copy-start(s32[1,16,1]{1,2,0:T(1,128)} %param.25) | copy-start | bytes 196
  20.7 26.6 %copy-start.4 = (bf16[256,2048]{1,0:T(8,128)(2,1)S(1)}, bf16[256,2048]{1,0:T(8,128)(2,1)}, u32[]{:S(2)}) copy-start(bf16[256,2048]{1,0:T(8,128)(2,1)} %refs_0_.3) | copy-start | bytes 3145732
  33.5 55.6 %collective-permute-start.2 = (bf16[256,2048]{1,0:T(8,128)(2,1)}, bf16[256,2048]{1,0:T(8,128)(2,1)}, u32[]{:S(2)}, u32[]{:S(2)}) collective-permute-start(bf16[256,2048]{1,0:T(8,128)(2,1)} %collective-permute-done.1), channel_id=1, source_target_pairs={{4,0},{8,4},{5,1},{9,5},{6,2},{10,6},{7,3},{11,7},{20,16},{24,20},... | collective-permute-start | bytes 3145736 | tf_op jit(solution)/shard_map/ppermute | solution.py:253
  36.3 37.2 %collective-permute-start.8 = (bf16[256,544]{1,0:T(8,128)(2,1)}, bf16[256,544]{1,0:T(8,128)(2,1)}, u32[]{:S(2)}, u32[]{:S(2)}) collective-permute-start(bf16[256,544]{1,0:T(8,128)(2,1)} %pad_maximum_fusion), channel_id=1, source_target_pairs={{0,12},{4,0},{8,4},{12,8},{1,13},{5,1},{9,5},{13,9},{2,14},{6,2},{... | collective-permute-start | bytes 835592 | tf_op jit(solution)/shard_map/ppermute | solution.py:242
  37.3 50.3 %collective-permute-start.7 = (bf16[256,544]{1,0:T(8,128)(2,1)}, bf16[256,544]{1,0:T(8,128)(2,1)}, u32[]{:S(2)}, u32[]{:S(2)}) collective-permute-start(bf16[256,544]{1,0:T(8,128)(2,1)} %pad_maximum_fusion), channel_id=1, source_target_pairs={{0,8},{4,12},{8,0},{12,4},{1,9},{5,13},{9,1},{13,5},{2,10},{6,14},... | collective-permute-start | bytes 835592 | tf_op jit(solution)/shard_map/ppermute | solution.py:242
  40.4 47.1 %collective-permute-start.6 = (bf16[256,544]{1,0:T(8,128)(2,1)}, bf16[256,544]{1,0:T(8,128)(2,1)}, u32[]{:S(2)}, u32[]{:S(2)}) collective-permute-start(bf16[256,544]{1,0:T(8,128)(2,1)} %pad_maximum_fusion), channel_id=1, source_target_pairs={{0,4},{4,8},{8,12},{12,0},{1,5},{5,9},{9,13},{13,1},{2,6},{6,10},{... | collective-permute-start | bytes 835592 | tf_op jit(solution)/shard_map/ppermute | solution.py:242
  50.9 39.7 %collective-permute-start.4 = (bf16[256,2048]{1,0:T(8,128)(2,1)}, bf16[256,2048]{1,0:T(8,128)(2,1)}, u32[]{:S(2)}, u32[]{:S(2)}) collective-permute-start(bf16[256,2048]{1,0:T(8,128)(2,1)} %collective-permute-done), channel_id=1, source_target_pairs={{4,8},{8,12},{5,9},{9,13},{6,10},{10,14},{7,11},{11,15},{20,24},{2... | collective-permute-start | bytes 3145736 | tf_op jit(solution)/shard_map/ppermute | solution.py:252
  89.1 45.5 %collective-permute-start.3 = (bf16[256,2048]{1,0:T(8,128)(2,1)}, bf16[256,2048]{1,0:T(8,128)(2,1)}, u32[]{:S(2)}, u32[]{:S(2)}) collective-permute-start(bf16[256,2048]{1,0:T(8,128)(2,1)} %collective-permute-done.2), channel_id=1, source_target_pairs={{4,0},{5,1},{6,2},{7,3},{20,16},{21,17},{22,18},{23,19}} | collective-permute-start | bytes 3145736 | tf_op jit(solution)/shard_map/ppermute | solution.py:253
  90.6 7.8 %slice-start = ((f32[256,544]{1,0:T(8,128)}), f32[256,32]{1,0:T(8,128)S(1)}, s32[]{:S(2)}) async-start(f32[256,544]{1,0:T(8,128)} %copy-done.13), calls=%async_computation.2 | async-start | bytes 262144 | tf_op jit(solution)/shard_map/slice | solution.py:314
  90.6 54.9 %all-to-all-start = ((bf16[4,256,512]{2,1,0:T(8,128)(2,1)}), bf16[4,256,512]{2,1,0:T(8,128)(2,1)}, u32[]{:S(2)}, u32[]{:S(2)}) async-start(bf16[4,256,512]{2,1,0:T(8,128)(2,1)} %bitcast.39), calls=%async_computation | async-start | bytes 2097152 | tf_op jit(solution)/shard_map/all_to_all | solution.py:325
  95.7 3.9 %copy-start.7 = (bf16[512,4096]{1,0:T(8,128)(2,1)S(1)}, bf16[512,4096]{1,0:T(8,128)(2,1)}, u32[]{:S(2)}) copy-start(bf16[512,4096]{1,0:T(8,128)(2,1)} %wdt_ref.1) | copy-start | bytes 12582916
  95.7 3.9 %copy-start.8 = (bf16[256,4096]{1,0:T(8,128)(2,1)S(1)}, bf16[256,4096]{1,0:T(8,128)(2,1)}, u32[]{:S(2)}) copy-start(bf16[256,4096]{1,0:T(8,128)(2,1)} %gate_ref.1) | copy-start | bytes 6291460
  95.7 3.9 %copy-start.9 = (f32[16,4096]{1,0:T(8,128)S(1)}, f32[16,4096]{1,0:T(8,128)}, u32[]{:S(2)}) copy-start(f32[16,4096]{1,0:T(8,128)} %alog_ref.1) | copy-start | bytes 786436
  95.7 3.9 %copy-start.10 = (f32[1,16,4096]{2,1,0:T(8,128)S(1)}, f32[1,16,4096]{2,1,0:T(8,128)}, u32[]{:S(2)}) copy-start(f32[1,16,4096]{2,1,0:T(8,128)} %param.29) | copy-start | bytes 786436
  95.7 3.9 %copy-start.11 = (f32[4096]{0:T(1024)S(1)}, f32[4096]{0:T(1024)}, u32[]{:S(2)}) copy-start(f32[4096]{0:T(1024)} %param.35) | copy-start | bytes 49156
  95.7 3.9 %copy-start.12 = (f32[4096]{0:T(1024)S(1)}, f32[4096]{0:T(1024)}, u32[]{:S(2)}) copy-start(f32[4096]{0:T(1024)} %param.37) | copy-start | bytes 49156
  95.8 40.3 %collective-permute-start.5 = (bf16[256,2048]{1,0:T(8,128)(2,1)}, bf16[256,2048]{1,0:T(8,128)(2,1)S(1)}, u32[]{:S(2)}, u32[]{:S(2)}) collective-permute-start(bf16[256,2048]{1,0:T(8,128)(2,1)} %collective-permute-done.4), channel_id=1, source_target_pairs={{8,12},{9,13},{10,14},{11,15},{24,28},{25,29},{26,30},{27,31}} | collective-permute-start | bytes 3145736 | tf_op jit(solution)/shard_map/ppermute | solution.py:252
  137.5 6.0 %copy-start.15 = (pred[4,16]{1,0:T(4,128)(4,1)S(1)}, pred[4,16]{1,0:T(4,128)(4,1)}, u32[]{:S(2)}) copy-start(pred[4,16]{1,0:T(4,128)(4,1)} %iota_compare_fusion.3) | copy-start | bytes 196
  145.5 40.3 %all-to-all-start.1 = ((bf16[4,8,8192]{2,1,0:T(8,128)(2,1)}), bf16[4,8,8192]{2,1,0:T(8,128)(2,1)}, u32[]{:S(2)}, u32[]{:S(2)}) async-start(bf16[4,8,8192]{2,1,0:T(8,128)(2,1)} %convolution_convert_fusion), calls=%async_computation.1 | async-start | bytes 1048576 | tf_op jit(solution)/shard_map/all_to_all | solution.py:370
  169.8 18.6 %copy-start.1 = (bf16[4096,32]{0,1:T(8,128)(2,1)S(1)}, bf16[4096,32]{0,1:T(8,128)(2,1)}, u32[]{:S(2)}) copy-start(bf16[4096,32]{0,1:T(8,128)(2,1)} %param.33) | copy-start | bytes 786436
  (5 other events, 7.9 us)

commit v3 on v2

--- a/solution.py
+++ b/solution.py
@@ -105,10 +105,10 @@
     )(bias, queries, cached, fresh)
 
 
-def scan_kernel(
-    norm_ref, spread_ref, wdt_ref, bias_ref, xconv_ref, gate_ref, alog_ref, skip_ref, init_ref,
-    out_ref, final_ref, step_s, push_s, read_s,
-):
+def scan_kernel(count, *refs):
+    norm_ref, spread_ref, wdt_ref, bias_ref, xconv_ref = refs[:5]
+    gate_ref, alog_ref, skip_ref, init_ref = refs[5:count]
+    out_ref, final_ref, step_s, push_s, read_s = refs[-5:]
     tokens, width = xconv_ref.shape
     states = alog_ref.shape[0]
     raw = jnp.dot(norm_ref[...], wdt_ref[...], preferred_element_type=jnp.float32) + bias_ref[...]
@@ -137,27 +137,27 @@
     out_ref[...] = (readout * (gate * jax.nn.sigmoid(gate))).astype(out_ref.dtype)
 
 
-def scan(low_norm, selection, w_dt, dt_bias, xconv, gate, a_log, d_skip, initial):
+def scan(low_norm, selection, w_dt, dt_bias, xconv, gate, a_log, d_skip, initial, late):
     tokens, channels = xconv.shape
     rank = low_norm.shape[1]
     states = a_log.shape[0]
     width = min(512, channels)
     spread = jnp.broadcast_to(selection[:, :, None], (tokens, 2 * states, 128))
-
-    def whole(shape):
-        return pl.BlockSpec(shape, lambda c: (0,) * len(shape))
-
-    def columns(rows):
-        return pl.BlockSpec((rows, width), lambda c: (0, c))
-
-    return pl.pallas_call(
-        scan_kernel,
-        grid=(channels // width,),
-        out_shape=(
-            jax.ShapeDtypeStruct((tokens, channels), jnp.bfloat16),
-            jax.ShapeDtypeStruct((states, channels), jnp.float32),
-        ),
-        in_specs=[
+    calls = 4 if channels // width >= 4 else 1
+    blocks = channels // width // calls
+    results = None
+    for call in range(calls):
+
+        def whole(shape):
+            return pl.BlockSpec(shape, lambda c: (0,) * len(shape))
+
+        def columns(rows, first=call * blocks):
+            return pl.BlockSpec((rows, width), lambda c: (0, first + c))
+
+        operands = [
+            late if call == 3 else low_norm, spread, w_dt, dt_bias[None, :], xconv, gate, a_log, d_skip[None, :], initial
+        ]
+        in_specs = [
             whole((tokens, rank)),
             whole((tokens, 2 * states, 128)),
             columns(rank),
@@ -167,18 +167,31 @@
             columns(states),
             columns(1),
             columns(states),
-        ],
-        out_specs=(columns(tokens), columns(states)),
-        scratch_shapes=[pltpu.VMEM((tokens, width), jnp.float32)] * 3,
-        compiler_params=pltpu.CompilerParams(vmem_limit_bytes=40 * MIB),
-        cost_estimate=pl.CostEstimate(
-            flops=2 * tokens * channels * rank + 7 * tokens * channels * states,
-            bytes_accessed=6 * tokens * channels + 2 * rank * channels + 12 * states * channels,
-            transcendentals=tokens * channels * states,
-        ),
-    )(
-        low_norm, spread, w_dt, dt_bias[None, :], xconv, gate, a_log, d_skip[None, :], initial
-    )
+        ]
+        aliases = {}
+        if results is not None:
+            aliases = {len(operands): 0, len(operands) + 1: 1}
+            operands += results
+            in_specs += [pl.BlockSpec(memory_space=pl.ANY)] * 2
+        results = pl.pallas_call(
+            functools.partial(scan_kernel, 9),
+            grid=(blocks,),
+            out_shape=(
+                jax.ShapeDtypeStruct((tokens, channels), jnp.bfloat16),
+                jax.ShapeDtypeStruct((states, channels), jnp.float32),
+            ),
+            in_specs=in_specs,
+            out_specs=(columns(tokens), columns(states)),
+            scratch_shapes=[pltpu.VMEM((tokens, width), jnp.float32)] * 3,
+            input_output_aliases=aliases,
+            compiler_params=pltpu.CompilerParams(vmem_limit_bytes=40 * MIB),
+            cost_estimate=pl.CostEstimate(
+                flops=2 * tokens * channels * rank // calls,
+                bytes_accessed=60 * MIB // calls,
+                transcendentals=tokens * channels * states // calls,
+            ),
+        )(*operands)
+    return results
 
 
 def project_kernel(count, has_sum, where_ref, *refs):
@@ -245,19 +258,11 @@
     return total
 
 
-def relay(own, size):
-    right = left = own
-    rights, lefts = [], []
-    for step in range(1, size):
-        right = lax.ppermute(right, "tp", [(t, t + 1) for t in range(step - 1, size - 1)])
-        left = lax.ppermute(left, "tp", [(t, t - 1) for t in range(1, size - step + 1)])
-        rights.append(right)
-        lefts.append(left)
-    me = lax.axis_index("tp")
-    found = [
-        jnp.where(me >= k, rights[k - 1], lefts[size - k - 1]) for k in range(1, size)
-    ]
-    return found, rights, lefts
+def pass_on(right, left, step, size):
+    return (
+        lax.ppermute(right, "tp", [(t, t + 1) for t in range(step - 1, size - 1)]),
+        lax.ppermute(left, "tp", [(t, t - 1) for t in range(1, size - step + 1)]),
+    )
 
 
 def body(
@@ -295,7 +300,7 @@
 
     line = tp_size == 4
     if line:
-        others, rights, lefts = relay(x_attn, tp_size)
+        first = pass_on(x_attn, x_attn, 1, tp_size)
 
     extended = jnp.concatenate([conv_prev[0], mamba_in], axis=0).astype(jnp.float32)
     convolved = jnp.broadcast_to(conv_bias[None, :], mamba_in.shape)
@@ -308,9 +313,10 @@
     select_part = jnp.dot(xconv, w_bc, preferred_element_type=jnp.float32)
     rank = w_xdt.shape[1]
     parts = jnp.concatenate([proj_part, select_part], axis=1).astype(jnp.bfloat16)
-    if line:
-        parts, _, _ = lax.optimization_barrier((parts, rights[0], lefts[0]))
     summed = exchange_sum(parts, tp_size)
+    if line:
+        *begun, summed = lax.optimization_barrier((*first, summed))
+        second = pass_on(*begun, 2, tp_size)
     projected, selection = summed[:, :rank], summed[:, rank:]
 
     local_slots = cache_pool.shape[1]
@@ -321,7 +327,7 @@
         outgoing_kv = jnp.repeat(pool, group_size // own_heads, axis=1)
     outgoing_kv = jnp.moveaxis(outgoing_kv, 1, 0)
     if line:
-        outgoing_kv, _, _ = lax.optimization_barrier((outgoing_kv, rights[1], lefts[1]))
+        outgoing_kv, _, _ = lax.optimization_barrier((outgoing_kv, *second))
     cached = lax.all_to_all(outgoing_kv, "tp", split_axis=0, concat_axis=0, tiled=True)
     cached = cached.reshape(tp_size * local_slots * PAGE, own_groups * head_cols)
     usable = token_usable(page_table[0], jnp.arange(page_table.shape[1]), cached_len[0])
@@ -332,7 +338,6 @@
     if line:
         fresh_sum = project([x_attn], [tp_index], w_keyval, kv_base, kv_own, None, jnp.float32)
         query_sum = project([x_attn], [tp_index], w_query, 0, w_query.shape[1], None, jnp.float32)
-        owners = [(tp_index + tp_size - k) % tp_size for k in range(1, tp_size)]
     else:
         fresh_sum = query_sum = None
         others = [lax.all_gather(x_attn, "tp", axis=1, tiled=True)]
@@ -341,11 +346,28 @@
         projected * lax.rsqrt(jnp.mean(projected * projected, axis=-1, keepdims=True) + 1e-06)
     ).astype(jnp.bfloat16)
     if line:
-        low_norm, _, _ = lax.optimization_barrier((low_norm, rights[1], lefts[1]))
+        late, *more = lax.optimization_barrier((low_norm, *second))
+        third = pass_on(*more, 3, tp_size)
+    else:
+        late = low_norm
     mamba_out, last_state = scan(
-        low_norm, selection, w_dt, dt_bias, xconv, gate_in, a_log, d_skip, state_prev[0]
-    )
-
+        low_norm, selection, w_dt, dt_bias, xconv, gate_in, a_log, d_skip, state_prev[0], late
+    )
+
+    if line:
+        blocks = (first, second, third)
+        others = [
+            jnp.where(tp_index >= k, blocks[k - 1][0], blocks[tp_size - k - 1][1])
+            for k in (2, 1, 3)
+        ]
+        owners = [(tp_index + tp_size - k) % tp_size for k in (2, 1, 3)]
+        fresh_sum = project(
+            others[:1], owners[:1], w_keyval, kv_base, kv_own, fresh_sum, jnp.float32
+        )
+        query_sum = project(
+            others[:1], owners[:1], w_query, 0, w_query.shape[1], query_sum, jnp.float32
+        )
+        others, owners = others[1:], owners[1:]
     fresh = project(others, owners, w_keyval, kv_base, kv_own, fresh_sum)
     queries = project(others, owners, w_query, 0, w_query.shape[1], query_sum)
 

time: 189 us -> 213 us (1.13)
  waiting for transfers between devices: 40.3 us -> 48 us
  local copies, waits for them, and re-layouts: 14.7 us -> 22.2 us
  Pallas kernels: 81.3 us -> 86.2 us
  starting transfers between devices: 29.9 us -> 34.6 us
    ppermute x3, waiting for transfers between devices: 27.5 us -> 36.3 us  [exchange_sum(): lax.ppermute(part, 'tp', [(t, (t + shift) % size) for t in range(size)])]
    unnamed x34 -> x46, local copies, waits for them, and re-layouts: 3.78 us -> 11.3 us
    all_to_all x1, starting transfers between devices: 6.57 us -> 11.3 us  [body(): lax.all_to_all(outgoing, 'tp', split_axis=0, concat_axis=2, tiled=True)]
    pallas_call x4 -> x6, Pallas kernels: 30.3 us -> 33 us  [project(): pl.pallas_call(functools.partial(project_kernel, count, so_far is not Non...]
    pallas_call x1 -> x4, Pallas kernels: 35 us -> 37.2 us  [scan(): pl.pallas_call(functools.partial(scan_kernel, 9), grid=(blocks,), out_sha...]
  transfers between devices with their start and end apart: 11 -> 11, of which waited for: 3 -> 3; matrix products, arithmetic and copies ran while one was open for 15% -> 13% of each run, Pallas kernels for 43% -> 41%
where the time goes in v3:
time: 213 us; the launch traced here: 212 us
  Pallas kernels  86.2 us (40%)
  waiting for transfers between devices  48 us (23%)
  starting transfers between devices  34.6 us (16%)
  local copies, waits for them, and re-layouts  22.2 us (10%)
  other arithmetic  12.9 us (6%)
  matrix products  6.18 us (3%)
    pallas_call x4, Pallas kernels, scan(): pl.pallas_call(functools.partial(scan_kernel, 9), grid=(blocks,), out_sha...  37.2 us
    ppermute x3, waiting for transfers between devices, exchange_sum(): lax.ppermute(part, 'tp', [(t, (t + shift) % size) for t in range(size)])  36.3 us
    pallas_call x6, Pallas kernels, project(): pl.pallas_call(functools.partial(project_kernel, count, so_far is not Non...  33 us
    pallas_call x1, Pallas kernels, attend(): pl.pallas_call(functools.partial(attention_kernel, chunk), grid=(own_grou...  16 us
    ppermute x3, waiting for transfers between devices, pass_on(): lax.ppermute(left, 'tp', [(t, t - 1) for t in range(1, size - step + 1)])  11.6 us
    unnamed x46, local copies, waits for them, and re-layouts  11.3 us
    all_to_all x1, starting transfers between devices, body(): lax.all_to_all(outgoing, 'tp', split_axis=0, concat_axis=2, tiled=True)  11.3 us
    ppermute x3, starting transfers between devices, pass_on(): lax.ppermute(right, 'tp', [(t, t + 1) for t in range(step - 1, size - 1)])  9.46 us
  transfers between devices with their start and end apart: 11, of which 3 were waited for; matrix products, arithmetic and copies ran while one was open for 13% of the time, Pallas kernels for 41%

profile of v3, /device:TPU:0, one launch (start us, length us, event | category | flops | bytes accessed | tf_op | source)
XLA Modules:
  0.0 211.6 jit_solution(14755916135571130041)
XLA Ops:
  0.7 6.2 %collective-permute-start = (bf16[256,2048]{1,0:T(8,128)(2,1)}, bf16[256,2048]{1,0:T(8,128)(2,1)}, u32[]{:S(2)}, u32[]{:S(2)}) collective-permute-start(bf16[256,2048]{1,0:T(8,128)(2,1)} %refs_0_.3), channel_id=1, source_target_pairs={{0,4},{4,8},{8,12},{1,5},{5,9},{9,13},{2,6},{6,10},{10,14},{3,7},{... | collective-permute-start | bytes 3145736 | tf_op jit(solution)/shard_map/ppermute | solution.py:263
  9.2 2.2 %maximum_convert_fusion = f32[259,4096]{1,0:T(8,128)S(1)} fusion(bf16[256,4096]{1,0:T(8,128)(2,1)} %param.26, bf16[3,4096]{1,0:T(4,128)(2,1)} %bitcast.53), kind=kLoop, calls=%fused_computation.10 | loop fusion | flops 4243456 | bytes 6365184 | tf_op jit(solution)/shard_map/convert_element_type | solution.py:305
  11.4 2.7 %multiply_convert_fusion.refs_4_ = bf16[256,4096]{1,0:T(8,128)(2,1)S(1)} fusion(f32[259,4096]{1,0:T(8,128)S(1)} %maximum_convert_fusion, f32[4096]{0:T(1024)S(1)} %bitcast.51, f32[4096]{0:T(1024)S(1)} %bitcast.52, f32[4096]{0:T(1024)S(1)} %bitcast.50, f32[4096]{0:T(1024)S(1)} %bitcast.49, f32[4096]{0:T(1024)S(1)} %copy-done.20), kind=kLoop, calls=%fused_computation.9 | loop fusion | flops 13631488 | bytes 18956288 | tf_op jit(solution)/shard_map/convert_element_type | solution.py:311
  15.0 3.4 %convolution_convert_fusion.1 = bf16[256,512]{1,0:T(8,128)(2,1)S(1)} fusion(bf16[256,4096]{1,0:T(8,128)(2,1)S(1)} %multiply_convert_fusion.refs_4_, bf16[4096,512]{1,0:T(8,128)(2,1)} %param.32), kind=kOutput, calls=%fused_computation.11 | convolution fusion | flops 1073872896 | bytes 6553600 | tf_op jit(solution)/shard_map/dot_general | solution.py:312
  19.2 4.6 %collective-permute-start.4 = (bf16[256,544]{1,0:T(8,128)(2,1)}, bf16[256,544]{1,0:T(8,128)(2,1)}, u32[]{:S(2)}, u32[]{:S(2)}) collective-permute-start(bf16[256,544]{1,0:T(8,128)(2,1)} %pad_maximum_fusion), channel_id=1, source_target_pairs={{0,12},{4,0},{8,4},{12,8},{1,13},{5,1},{9,5},{13,9},{2,14},{6,2},{... | collective-permute-start | bytes 835592 | tf_op jit(solution)/shard_map/ppermute | solution.py:255
  25.3 16.2 %collective-permute-done.4 = bf16[256,544]{1,0:T(8,128)(2,1)} collective-permute-done((bf16[256,544]{1,0:T(8,128)(2,1)}, bf16[256,544]{1,0:T(8,128)(2,1)}, u32[]{:S(2)}, u32[]{:S(2)}) %collective-permute-start.4) | collective-permute-done | bytes 278560 | tf_op jit(solution)/shard_map/ppermute | solution.py:255
  41.5 20.2 %collective-permute-done.3 = bf16[256,544]{1,0:T(8,128)(2,1)} collective-permute-done((bf16[256,544]{1,0:T(8,128)(2,1)}, bf16[256,544]{1,0:T(8,128)(2,1)}, u32[]{:S(2)}, u32[]{:S(2)}) %collective-permute-start.3) | collective-permute-done | bytes 278560 | tf_op jit(solution)/shard_map/ppermute | solution.py:255
  67.0 2.6 %reshape_reshape_squeeze.3 = bf16[256,4,512]{2,1,0:T(4,128)(2,1)} reshape(bf16[1,16,16,2048]{3,2,1,0:T(8,128)(2,1)} %param.22) | data formatting | bytes 2097152 | tf_op jit(solution)/shard_map/reshape;reshape;squeeze | solution.py:325
  69.6 2.4 %copy.42 = bf16[256,4,512]{2,0,1:T(8,128)(2,1)} copy(bf16[256,4,512]{2,1,0:T(4,128)(2,1)} %reshape_reshape_squeeze.3) | data formatting | bytes 2097152 | tf_op jit(solution)/shard_map/reshape;reshape;squeeze | solution.py:325
  72.0 6.2 %shard_map.210.refs_2_ = f32[256,2048]{1,0:T(8,128)S(1)} custom-call(s32[2]{0:T(128)S(1)} %get-tuple-element.42.where_ref, bf16[256,2048]{1,0:T(8,128)(2,1)S(1)} %copy-done.14, bf16[8192,2048]{1,0:T(8,128)(2,1)} %refs_2_.6), custom_call_target="tpu_custom_call" | custom-call | flops 2147483648 | bytes 11534336 | tf_op jit(solution)/shard_map/pallas_call | solution.py:231
  79.8 11.6 %collective-permute-done.6 = bf16[256,2048]{1,0:T(8,128)(2,1)} collective-permute-done((bf16[256,2048]{1,0:T(8,128)(2,1)}, bf16[256,2048]{1,0:T(8,128)(2,1)}, u32[]{:S(2)}, u32[]{:S(2)}) %collective-permute-start.6) | collective-permute-done | bytes 1048608 | tf_op jit(solution)/shard_map/ppermute | solution.py:264
  92.7 3.0 %shard_map.213.refs_2_ = f32[256,512]{1,0:T(8,128)S(1)} custom-call(s32[2]{0:T(128)S(1)} %get-tuple-element.43.where_ref, bf16[256,2048]{1,0:T(8,128)(2,1)S(1)} %copy-done.14, bf16[8192,2048]{1,0:T(8,128)(2,1)} %refs_2_.7), custom_call_target="tpu_custom_call" | custom-call | flops 536870912 | bytes 3670016 | tf_op jit(solution)/shard_map/pallas_call | solution.py:231
  98.8 9.3 %shard_map.217 = (bf16[256,4096]{1,0:T(8,128)(2,1)}, f32[16,4096]{1,0:T(8,128)}) custom-call(bf16[256,512]{1,0:T(8,128)(2,1)S(1)} %multiply_convert_fusion.1.refs_0_, f32[256,32,128]{2,1,0:T(8,128)S(1)} %broadcast_in_dim.35.refs_1_, bf16[512,4096]{1,0:T(8,128)(2,1)S(1)} %copy-done.4, f32[1,4096]{1,0:T(1,128)S(1)} %bitcast.40, ...), custom_call_target="tpu_custom_call" | custom-call | flops 268435456 | bytes 15728640 | tf_op jit(solution)/shard_map/pallas_call | solution.py:176
  108.1 9.3 %shard_map.218 = (bf16[256,4096]{1,0:T(8,128)(2,1)}, f32[16,4096]{1,0:T(8,128)}) custom-call(bf16[256,512]{1,0:T(8,128)(2,1)S(1)} %multiply_convert_fusion.1.refs_0_, f32[256,32,128]{2,1,0:T(8,128)S(1)} %broadcast_in_dim.35.refs_1_, bf16[512,4096]{1,0:T(8,128)(2,1)S(1)} %copy-done.4, ...), custom_call_target="tpu_custom_call", output_to_operand_aliasing={{0}: (9, {}), {1}: (10, {})} | custom-call | flops 268435456 | bytes 15728640 | tf_op jit(solution)/shard_map/pallas_call | solution.py:176
  117.4 9.3 %shard_map.219 = (bf16[256,4096]{1,0:T(8,128)(2,1)}, f32[16,4096]{1,0:T(8,128)}) custom-call(bf16[256,512]{1,0:T(8,128)(2,1)S(1)} %multiply_convert_fusion.1.refs_0_, f32[256,32,128]{2,1,0:T(8,128)S(1)} %broadcast_in_dim.35.refs_1_, bf16[512,4096]{1,0:T(8,128)(2,1)S(1)} %copy-done.4, ...), custom_call_target="tpu_custom_call", output_to_operand_aliasing={{0}: (9, {}), {1}: (10, {})} | custom-call | flops 268435456 | bytes 15728640 | tf_op jit(solution)/shard_map/pallas_call | solution.py:176
  128.3 4.9 %all-to-all-start = ((bf16[4,256,512]{2,1,0:T(8,128)(2,1)}), bf16[4,256,512]{2,1,0:T(8,128)(2,1)}, u32[]{:S(2)}, u32[]{:S(2)}) async-start(bf16[4,256,512]{2,1,0:T(8,128)(2,1)} %bitcast.34), calls=%async_computation | async-start | bytes 2097152 | tf_op jit(solution)/shard_map/all_to_all | solution.py:331
  135.1 2.2 %copy-done.3 = f32[256,32,128]{2,1,0:T(8,128)S(1)} copy-done((f32[256,32,128]{2,1,0:T(8,128)S(1)}, f32[256,32,128]{2,1,0:T(8,128)}, u32[]{:S(2)}) %copy-start.3) | copy-done | bytes 4194328
  141.4 9.3 %shard_map.220 = (bf16[256,4096]{1,0:T(8,128)(2,1)}, f32[16,4096]{1,0:T(8,128)}) custom-call(bf16[256,512]{1,0:T(8,128)(2,1)S(1)} %multiply_convert_fusion.1.refs_0_, f32[256,32,128]{2,1,0:T(8,128)S(1)} %copy-done.3, bf16[512,4096]{1,0:T(8,128)(2,1)S(1)} %copy-done.5, f32[1,4096]{1,0:T(1,128)S(1)} %bitcast.43, ...), custom_call_target="tpu_custom_call", output_to_operand_aliasing={{0}: (9, {}), {1}: (10, {})} | custom-call | flops 268435456 | bytes 15728640 | tf_op jit(solution)/shard_map/pallas_call | solution.py:176
  150.7 2.8 %shard_map.214.refs_3_ = f32[256,512]{1,0:T(8,128)S(1)} custom-call(s32[2]{0:T(128)S(1)} %get-tuple-element.41.where_ref, bf16[256,2048]{1,0:T(8,128)(2,1)S(1)} %broadcast_select_fusion.refs_0_, bf16[8192,2048]{1,0:T(8,128)(2,1)} %refs_2_.7, f32[256,512]{1,0:T(8,128)S(1)} %copy-done.16), custom_call_target="tpu_custom_call" | custom-call | flops 536870912 | bytes 3670016 | tf_op jit(solution)/shard_map/pallas_call | solution.py:231
  156.3 3.6 %shard_map.215.fresh_ref = bf16[256,512]{1,0:T(8,128)(2,1)S(1)} custom-call(s32[3]{0:T(128)S(1)} %get-tuple-element.39.where_ref, bf16[256,2048]{1,0:T(8,128)(2,1)S(1)} %broadcast_select_fusion.2.refs_0_, bf16[256,2048]{1,0:T(8,128)(2,1)S(1)} %broadcast_select_fusion.1.refs_1_, bf16[8192,2048]{1,0:T(8,128)(2,1)} %refs_2_.7, f32[256,512]{1,0:T(8,128)S(1)} %shard_map.214.refs_3_), custom_call_target="tpu_custom_call" | custom-call | flops 1073741824 | bytes 6815744 | tf_op jit(solution)/shard_map/pallas_call | solution.py:231
  162.7 11.3 %all-to-all-start.1 = ((bf16[4,8,8192]{2,1,0:T(8,128)(2,1)}), bf16[4,8,8192]{2,1,0:T(8,128)(2,1)}, u32[]{:S(2)}, u32[]{:S(2)}) async-start(bf16[4,8,8192]{2,1,0:T(8,128)(2,1)} %convolution_convert_fusion), calls=%async_computation.1 | async-start | bytes 1048576 | tf_op jit(solution)/shard_map/all_to_all | solution.py:392
  175.6 6.2 %shard_map.211.refs_3_ = f32[256,2048]{1,0:T(8,128)S(1)} custom-call(s32[2]{0:T(128)S(1)} %get-tuple-element.40.where_ref, bf16[256,2048]{1,0:T(8,128)(2,1)S(1)} %broadcast_select_fusion.refs_0_, bf16[8192,2048]{1,0:T(8,128)(2,1)} %refs_2_.6, f32[256,2048]{1,0:T(8,128)S(1)} %copy-done.9), custom_call_target="tpu_custom_call" | custom-call | flops 2147483648 | bytes 11534336 | tf_op jit(solution)/shard_map/pallas_call | solution.py:231
  181.8 11.2 %shard_map.212.query_ref = bf16[256,2048]{1,0:T(8,128)(2,1)S(1)} custom-call(s32[3]{0:T(128)S(1)} %get-tuple-element.38.where_ref, bf16[256,2048]{1,0:T(8,128)(2,1)S(1)} %broadcast_select_fusion.2.refs_0_, bf16[256,2048]{1,0:T(8,128)(2,1)S(1)} %broadcast_select_fusion.1.refs_1_, bf16[8192,2048]{1,0:T(8,128)(2,1)} %refs_2_.6, f32[256,2048]{1,0:T(8,128)S(1)} %shard_map.211.refs_3_), custom_call_target="tpu_custom_call" | custom-call | flops 4294967296 | bytes 20971520 | tf_op jit(solution)/shard_map/pallas_call | solution.py:231
  193.0 16.0 %shard_map.216 = bf16[256,2048]{1,0:T(8,128)(2,1)} custom-call(f32[1,1024]{1,0:T(1,128)S(1)} %select_n.63.bias_ref, bf16[256,2048]{1,0:T(8,128)(2,1)S(1)} %shard_map.212.query_ref, bf16[1024,512]{1,0:T(8,128)(2,1)} %bitcast.12.cached_ref, bf16[256,512]{1,0:T(8,128)(2,1)S(1)} %shard_map.215.fresh_ref), custom_call_target="tpu_custom_call" | custom-call | flops 2684354560 | bytes 3145728 | tf_op jit(solution)/shard_map/pallas_call | solution.py:88
  (88 shorter events, 33.5 us)
Async XLA Ops:
  0.6 13.5 %copy-start = (bf16[4096,32]{0,1:T(8,128)(2,1)S(1)}, bf16[4096,32]{0,1:T(8,128)(2,1)}, u32[]{:S(2)}) copy-start(bf16[4096,32]{0,1:T(8,128)(2,1)} %param.33) | copy-start | bytes 786436
  0.6 10.7 %copy-start.20 = (f32[4096]{0:T(1024)S(1)}, f32[4096]{0:T(1024)}, u32[]{:S(2)}) copy-start(f32[4096]{0:T(1024)} %param.31) | copy-start | bytes 49156
  0.7 63.2 %collective-permute-start = (bf16[256,2048]{1,0:T(8,128)(2,1)}, bf16[256,2048]{1,0:T(8,128)(2,1)}, u32[]{:S(2)}, u32[]{:S(2)}) collective-permute-start(bf16[256,2048]{1,0:T(8,128)(2,1)} %refs_0_.3), channel_id=1, source_target_pairs={{0,4},{4,8},{8,12},{1,5},{5,9},{9,13},{2,6},{6,10},{10,14},{3,7},{... | collective-permute-start | bytes 3145736 | tf_op jit(solution)/shard_map/ppermute | solution.py:263
  6.8 57.0 %collective-permute-start.1 = (bf16[256,2048]{1,0:T(8,128)(2,1)}, bf16[256,2048]{1,0:T(8,128)(2,1)}, u32[]{:S(2)}, u32[]{:S(2)}) collective-permute-start(bf16[256,2048]{1,0:T(8,128)(2,1)} %refs_0_.3), channel_id=1, source_target_pairs={{4,0},{8,4},{12,8},{5,1},{9,5},{13,9},{6,2},{10,6},{14,10},{7,3},{... | collective-permute-start | bytes 3145736 | tf_op jit(solution)/shard_map/ppermute | solution.py:264
  15.0 9.4 %copy-start.21 = (s32[1,64]{1,0:T(1,128)S(1)}, s32[1,64]{1,0:T(1,128)}, u32[]{:S(2)}) copy-start(s32[1,64]{1,0:T(1,128)} %param.23) | copy-start | bytes 772
  18.4 53.6 %copy-start.14 = (bf16[256,2048]{1,0:T(8,128)(2,1)S(1)}, bf16[256,2048]{1,0:T(8,128)(2,1)}, u32[]{:S(2)}) copy-start(bf16[256,2048]{1,0:T(8,128)(2,1)} %refs_0_.3) | copy-start | bytes 3145732
  19.2 22.3 %collective-permute-start.4 = (bf16[256,544]{1,0:T(8,128)(2,1)}, bf16[256,544]{1,0:T(8,128)(2,1)}, u32[]{:S(2)}, u32[]{:S(2)}) collective-permute-start(bf16[256,544]{1,0:T(8,128)(2,1)} %pad_maximum_fusion), channel_id=1, source_target_pairs={{0,12},{4,0},{8,4},{12,8},{1,13},{5,1},{9,5},{13,9},{2,14},{6,2},{... | collective-permute-start | bytes 835592 | tf_op jit(solution)/shard_map/ppermute | solution.py:255
  23.7 37.9 %collective-permute-start.3 = (bf16[256,544]{1,0:T(8,128)(2,1)}, bf16[256,544]{1,0:T(8,128)(2,1)}, u32[]{:S(2)}, u32[]{:S(2)}) collective-permute-start(bf16[256,544]{1,0:T(8,128)(2,1)} %pad_maximum_fusion), channel_id=1, source_target_pairs={{0,8},{4,12},{8,0},{12,4},{1,9},{5,13},{9,1},{13,5},{2,10},{6,14},... | collective-permute-start | bytes 835592 | tf_op jit(solution)/shard_map/ppermute | solution.py:255
  23.8 37.9 %collective-permute-start.2 = (bf16[256,544]{1,0:T(8,128)(2,1)}, bf16[256,544]{1,0:T(8,128)(2,1)}, u32[]{:S(2)}, u32[]{:S(2)}) collective-permute-start(bf16[256,544]{1,0:T(8,128)(2,1)} %pad_maximum_fusion), channel_id=1, source_target_pairs={{0,4},{4,8},{8,12},{12,0},{1,5},{5,9},{9,13},{13,1},{2,6},{6,10},{... | collective-permute-start | bytes 835592 | tf_op jit(solution)/shard_map/ppermute | solution.py:255
  63.8 16.0 %collective-permute-start.5 = (bf16[256,2048]{1,0:T(8,128)(2,1)}, bf16[256,2048]{1,0:T(8,128)(2,1)}, u32[]{:S(2)}, u32[]{:S(2)}) collective-permute-start(bf16[256,2048]{1,0:T(8,128)(2,1)} %collective-permute-done), channel_id=1, source_target_pairs={{4,8},{8,12},{5,9},{9,13},{6,10},{10,14},{7,11},{11,15},{20,24},{2... | collective-permute-start | bytes 3145736 | tf_op jit(solution)/shard_map/ppermute | solution.py:263
  65.5 25.9 %collective-permute-start.6 = (bf16[256,2048]{1,0:T(8,128)(2,1)}, bf16[256,2048]{1,0:T(8,128)(2,1)}, u32[]{:S(2)}, u32[]{:S(2)}) collective-permute-start(bf16[256,2048]{1,0:T(8,128)(2,1)} %collective-permute-done.1), channel_id=1, source_target_pairs={{4,0},{8,4},{5,1},{9,5},{6,2},{10,6},{7,3},{11,7},{20,16},{24,20},... | collective-permute-start | bytes 3145736 | tf_op jit(solution)/shard_map/ppermute | solution.py:264
  72.0 7.6 %copy-start.22 = (s32[1,16,1]{1,2,0:T(1,128)S(1)}, s32[1,16,1]{1,2,0:T(1,128)}, u32[]{:S(2)}) copy-start(s32[1,16,1]{1,2,0:T(1,128)} %param.25) | copy-start | bytes 196
  72.0 7.6 %copy-start.19 = (f32[256,544]{1,0:T(8,128)S(1)}, f32[256,544]{1,0:T(8,128)}, u32[]{:S(2)}) copy-start(f32[256,544]{1,0:T(8,128)} %convert_add_fusion) | copy-start | bytes 1671172
  91.4 62.1 %collective-permute-start.7 = (bf16[256,2048]{1,0:T(8,128)(2,1)}, bf16[256,2048]{1,0:T(8,128)(2,1)}, u32[]{:S(2)}, u32[]{:S(2)}) collective-permute-start(bf16[256,2048]{1,0:T(8,128)(2,1)} %collective-permute-done.6), channel_id=1, source_target_pairs={{4,0},{5,1},{6,2},{7,3},{20,16},{21,17},{22,18},{23,19}} | collective-permute-start | bytes 3145736 | tf_op jit(solution)/shard_map/ppermute | solution.py:264
  92.7 4.1 %slice-start = ((f32[256,544]{1,0:T(8,128)}), f32[256,32]{1,0:T(8,128)S(1)}, s32[]{:S(2)}) async-start(f32[256,544]{1,0:T(8,128)} %convert_add_fusion), calls=%async_computation.2 | async-start | bytes 262144 | tf_op jit(solution)/shard_map/slice | solution.py:320
  92.7 5.2 %copy-start.6 = (bf16[256,4096]{1,0:T(8,128)(2,1)S(1)}, bf16[256,4096]{1,0:T(8,128)(2,1)}, u32[]{:S(2)}) copy-start(bf16[256,4096]{1,0:T(8,128)(2,1)} %refs_5_.7) | copy-start | bytes 6291460
  92.7 5.2 %copy-start.12 = (f32[1,16,4096]{2,1,0:T(8,128)S(1)}, f32[1,16,4096]{2,1,0:T(8,128)}, u32[]{:S(2)}) copy-start(f32[1,16,4096]{2,1,0:T(8,128)} %param.29) | copy-start | bytes 786436
  96.6 2.2 %copy-start.18 = (f32[4096]{0:T(1024)S(1)}, f32[4096]{0:T(1024)}, u32[]{:S(2)}) copy-start(f32[4096]{0:T(1024)} %param.37) | copy-start | bytes 49156
  97.9 19.5 %copy-start.2 = (f32[256,32,128]{2,1,0:T(8,128)}, f32[256,32,128]{2,1,0:T(8,128)S(1)}, u32[]{:S(2)}) copy-start(f32[256,32,128]{2,1,0:T(8,128)S(1)} %broadcast_in_dim.35.refs_1_) | copy-start | bytes 12582916
  126.7 28.2 %collective-permute-start.8 = (bf16[256,2048]{1,0:T(8,128)(2,1)}, bf16[256,2048]{1,0:T(8,128)(2,1)}, u32[]{:S(2)}, u32[]{:S(2)}) collective-permute-start(bf16[256,2048]{1,0:T(8,128)(2,1)} %collective-permute-done.5), channel_id=1, source_target_pairs={{8,12},{9,13},{10,14},{11,15},{24,28},{25,29},{26,30},{27,31}} | collective-permute-start | bytes 3145736 | tf_op jit(solution)/shard_map/ppermute | solution.py:263
  128.3 34.4 %all-to-all-start = ((bf16[4,256,512]{2,1,0:T(8,128)(2,1)}), bf16[4,256,512]{2,1,0:T(8,128)(2,1)}, u32[]{:S(2)}, u32[]{:S(2)}) async-start(bf16[4,256,512]{2,1,0:T(8,128)(2,1)} %bitcast.34), calls=%async_computation | async-start | bytes 2097152 | tf_op jit(solution)/shard_map/all_to_all | solution.py:331
  141.4 9.3 %copy-start.16 = (f32[256,512]{1,0:T(8,128)S(1)}, f32[256,512]{1,0:T(8,128)}, u32[]{:S(2)}) copy-start(f32[256,512]{1,0:T(8,128)} %copy-done.15) | copy-start | bytes 1572868
  162.7 46.3 %all-to-all-start.1 = ((bf16[4,8,8192]{2,1,0:T(8,128)(2,1)}), bf16[4,8,8192]{2,1,0:T(8,128)(2,1)}, u32[]{:S(2)}, u32[]{:S(2)}) async-start(bf16[4,8,8192]{2,1,0:T(8,128)(2,1)} %convolution_convert_fusion), calls=%async_computation.1 | async-start | bytes 1048576 | tf_op jit(solution)/shard_map/all_to_all | solution.py:392
  193.0 18.6 %copy-start.1 = (bf16[4096,32]{0,1:T(8,128)(2,1)S(1)}, bf16[4096,32]{0,1:T(8,128)(2,1)}, u32[]{:S(2)}) copy-start(bf16[4096,32]{0,1:T(8,128)(2,1)} %param.33) | copy-start | bytes 786436
  (11 other events, 18.6 us)
